TPU v7x, 128 devices: a whole 4x4x4 slice. The times are simulated.
128 devices in a mesh: group: 2 (over core), tok: 4 (over x), vocab: 16 (over y, z).
Axes of the slice: x: 4, y: 4, z: 4, core: 2. Of those that a mesh axis runs over, the one named last changes fastest.
Arguments:
- teacher_hidden: bfloat16 [8192, 8192], P('tok', ('group', 'vocab')), may hold values from -160 to 160
- student_hidden: bfloat16 [8192, 5120], P('tok', ('group', 'vocab')), may hold values from -160 to 160
- teacher_gain: bfloat16 [8192], P(('group', 'vocab')), may hold values from 0.099609375 to 1.8984375
- student_gain: bfloat16 [5120], P(('group', 'vocab')), may hold values from 0.099609375 to 1.8984375
- teacher_head: bfloat16 [8192, 98304], P(None, ('group', 'tok', 'vocab')), may hold values from -10 to 10
- student_head: bfloat16 [5120, 98304], P(None, ('group', 'tok', 'vocab')), may hold values from -10 to 10
- targets: int32 [8192], replicated, may hold values from 0 to 98303
- mask_positions: int32 [1024], replicated, may hold values from 0 to 2047, as said below
- mask_counts: int32 [4], replicated, may hold values from 1 to 256, as said below
- mask_time: int32 [1], replicated, may hold values from 250 to 1000
Outputs:
- slot_kl: float32 [1024], P('tok')
- slot_nll: float32 [1024], P('tok')
- losses: float32 [2], replicated
Inputs may be any that keep to these rules, and one draw needn't show every extreme that they name: `mask_positions`: entries t * 256 to (t + 1) * 256 - 1 are distinct positions within tok shard t's 2048 tokens; only the first mask_counts[t] of them are masked, the others carry no weight. `mask_counts`: one shard has exactly 256; all shards together have exactly 512.
All inputs are finite; a program needn't handle non-finite values.
Results may differ from a plain program's by a relative error of at most 0.00071.
Values may be sent and summed in bfloat16 or wider, within the bound.
A program may use at most 192 MiB of HBM per device.

v0:
```python
import jax
import jax.numpy as jnp
from jax import lax
from jax.sharding import PartitionSpec as P

EPS = 1e-06


def normalize_rows(hidden_float, square_sums, width, feature_gain):
    scaled = (
        hidden_float
        * lax.rsqrt(square_sums / width + EPS)[:, None]
        * feature_gain.astype(jnp.float32)[None, :]
    )
    return scaled.astype(jnp.bfloat16)


def shards(
    teacher_hidden,
    student_hidden,
    teacher_gain,
    student_gain,
    teacher_head,
    student_head,
    targets,
    mask_positions,
    mask_counts,
    mask_time,
):
    shard_total = lax.axis_size("tok")
    shard_rows = teacher_hidden.shape[0]
    slot_total = mask_positions.shape[0]
    shard_slots = slot_total // shard_total
    vocab_width = teacher_head.shape[1]
    my_shard = lax.axis_index("tok")
    my_positions = lax.dynamic_slice_in_dim(mask_positions, my_shard * shard_slots, shard_slots)
    picked_teacher = jnp.take(teacher_hidden, my_positions, axis=0)
    picked_student = jnp.take(student_hidden, my_positions, axis=0)
    slot_index = jnp.arange(slot_total, dtype=jnp.int32)
    shard_index = slot_index // shard_slots
    row_live = slot_index % shard_slots < mask_counts[shard_index]
    token_index = shard_index * shard_rows + mask_positions[slot_index]
    target_ids = jnp.take(targets, token_index)
    rows_teacher, rows_student = (
        lax.all_gather(picked_teacher, "tok", axis=0, tiled=True),
        lax.all_gather(picked_student, "tok", axis=0, tiled=True),
    )
    teacher_float = rows_teacher.astype(jnp.float32)
    student_float = rows_student.astype(jnp.float32)
    square_teacher, square_student = lax.psum(
        (
            jnp.sum(teacher_float * teacher_float, axis=1),
            jnp.sum(student_float * student_float, axis=1),
        ),
        ("group", "vocab"),
    )
    normed_teacher = normalize_rows(
        teacher_float, square_teacher, teacher_head.shape[0], teacher_gain
    )
    normed_student = normalize_rows(
        student_float, square_student, student_head.shape[0], student_gain
    )
    weights = teacher_head
    logit_teacher = jnp.dot(
        lax.all_gather(normed_teacher, ("group", "vocab"), axis=1, tiled=True),
        weights,
        preferred_element_type=jnp.float32,
    )
    weights = student_head
    logit_student = jnp.dot(
        lax.all_gather(normed_student, ("group", "vocab"), axis=1, tiled=True),
        weights,
        preferred_element_type=jnp.float32,
    )
    first_entry = lax.axis_index(("group", "tok", "vocab")) * vocab_width
    top_teacher = jnp.max(logit_teacher, axis=1)
    top_student = jnp.max(logit_student, axis=1)
    weight_teacher = jnp.exp(logit_teacher - top_teacher[:, None])
    mass_teacher = jnp.sum(weight_teacher, axis=1)
    mass_student = jnp.sum(jnp.exp(logit_student - top_student[:, None]), axis=1)
    cross_term = jnp.sum(weight_teacher * (logit_teacher - logit_student), axis=1)
    target_hit = (target_ids - first_entry)[:, None] == jnp.arange(vocab_width, dtype=jnp.int32)[
        None, :
    ]
    target_logit = jnp.sum(jnp.where(target_hit, logit_student, 0.0), axis=1)
    peak_teacher, peak_student = lax.pmax((top_teacher, top_student), ("group", "tok", "vocab"))
    shift_teacher = jnp.exp(top_teacher - peak_teacher)
    shift_student = jnp.exp(top_student - peak_student)
    mass_teacher, mass_student, cross_term, target_logit = lax.psum(
        (
            mass_teacher * shift_teacher,
            mass_student * shift_student,
            cross_term * shift_teacher,
            target_logit,
        ),
        ("group", "tok", "vocab"),
    )
    lse_teacher = peak_teacher + jnp.log(mass_teacher)
    lse_student = peak_student + jnp.log(mass_student)
    row_kl = cross_term / mass_teacher - lse_teacher + lse_student
    row_nll = lse_student - target_logit
    lookup = my_shard * shard_slots + jnp.arange(shard_slots, dtype=jnp.int32)
    mine_live = jnp.arange(shard_slots, dtype=jnp.int32) < mask_counts[my_shard]
    slot_kl = jnp.where(mine_live, row_kl[lookup], 0.0)
    slot_nll = jnp.where(mine_live, row_nll[lookup], 0.0)
    weight = 1000.0 / mask_time[0].astype(jnp.float32)
    nll_total = jnp.sum(jnp.where(row_live, row_nll, 0.0))
    kl_total = jnp.sum(jnp.where(row_live, row_kl, 0.0))
    masked_total = jnp.sum(mask_counts).astype(jnp.float32)
    losses = jnp.stack([weight * nll_total / (shard_rows * shard_total), kl_total / masked_total])
    return (slot_kl, slot_nll, losses)


def solution(mesh):
    in_specs = (
        P("tok", ("group", "vocab")),
        P("tok", ("group", "vocab")),
        P(("group", "vocab")),
        P(("group", "vocab")),
        P(None, ("group", "tok", "vocab")),
        P(None, ("group", "tok", "vocab")),
        P(),
        P(),
        P(),
        P(),
    )
    out_specs = (P("tok"), P("tok"), P())
    return jax.shard_map(shards, mesh=mesh, in_specs=in_specs, out_specs=out_specs, check_vma=False)
```

profile of v0, /device:TPU:0, one launch (start us, length us, event | category | flops | bytes accessed | tf_op | source)
XLA Modules:
  0.0 414.7 jit_solution(14169006355810576995)
XLA Ops:
  7.2 0.0 copy-start
  7.2 0.0 all-gather.5.cloned.1.call-start
  7.2 0.8 compare_and_fusion
  8.1 0.0 copy-start.4
  8.1 1.4 copy.17
  9.5 0.0 copy-start.5
  9.5 1.2 gather_fusion.1
  10.7 0.0 copy-start.1
  10.7 0.1 copy.18
  10.8 12.8 %all_gather.14 = bf16[1024,160]{0,1:T(8,128)(2,1)S(1)} all-gather(bf16[256,160]{0,1:T(8,128)(2,1)S(1)} %broadcast_select_fusion.1), channel_id=1, replica_groups=mesh['group'=2,'tok'=4,'vocab'=16] {'tok'}, dimensions={0}, use_global_device_ids=true | all-gather | bytes 409600 | tf_op jit(solution)/shard_map/all_gather | solution.py:46
  23.6 0.1 fusion.4
  23.7 0.0 copy-done
  23.7 1.2 gather_fusion
  24.9 0.1 broadcast_select_fusion
  25.0 12.8 %all_gather.12 = bf16[1024,256]{1,0:T(8,128)(2,1)S(1)} all-gather(bf16[256,256]{1,0:T(8,128)(2,1)S(1)} %broadcast_select_fusion), channel_id=1, replica_groups=mesh['group'=2,'tok'=4,'vocab'=16] {'tok'}, dimensions={0}, use_global_device_ids=true | all-gather | bytes 655360 | tf_op jit(solution)/shard_map/all_gather | solution.py:45
  37.8 0.2 fusion.1
  38.0 65.6 %all-reduce.2 = (f32[1024]{0:T(1024)S(1)}, f32[1024]{0:T(1024)S(1)}) all-reduce(f32[1024]{0:T(1024)S(1)} %fusion.1, f32[1024]{0:T(1024)S(1)} %fusion.4), channel_id=1, replica_groups=mesh['group'=2,'tok'=4,'vocab'=16] {'group','vocab'}, use_global_device_ids=true, to_apply=%region_1.2 | all-reduce | flops 2048 | bytes 16384 | tf_op jit(solution)/shard_map/psum | solution.py:50
  103.6 0.0 copy-done.4
  103.7 0.8 fusion.6
  104.5 0.0 copy-start.3
  104.5 0.0 copy-start.2
  104.5 0.0 all-gather.5.cloned.1.call-update
  104.5 0.0 all-gather.3.cloned.1.call-start
  104.6 0.0 copy-done.5
  104.6 1.0 fusion.3
  105.6 0.0 all-gather.3.cloned.1.call-update
  105.6 0.0 copy-done.1
  105.7 4.7 %gather_fusion.3 = s32[1024]{0:T(1024)S(1)} fusion(s32[1024]{0:T(1024)S(1)} %copy-done.1, s32[1024]{0:T(1024)S(1)} %iota_clamp_fusion), kind=kCustom, calls=%fused_computation.3 | custom fusion | bytes 12288 | tf_op jit(solution)/shard_map/gather | solution.py:42
  111.0 0.0 copy-done.3
  111.0 0.6 reduce_sum.89
  112.4 0.0 copy-done.2
  112.4 6.2 %gather_fusion.4 = s32[1024]{0:T(1024)S(1)} fusion(s32[8192]{0:T(1024)S(1)} %copy-done.2, s32[1024]{0:T(1024)S(1)} %broadcast_clamp_fusion), kind=kCustom, calls=%fused_computation.4 | custom fusion | bytes 12288 | tf_op jit(solution)/shard_map/jit(_take)/gather | solution.py:43
  118.6 0.6 fusion.23
  119.2 2.5 compare_select_fusion.2
  121.7 41.0 %all-gather.5.cloned.1.call-done = bf16[1024,5120]{0,1:T(8,128)(2,1)} async-done(((bf16[1024,160]{0,1:T(8,128)(2,1)}), bf16[1024,5120]{0,1:T(8,128)(2,1)}) %all-gather.5.cloned.1.call-update) | async-done | bytes 10485776 | tf_op jit(solution)/shard_map/all_gather | solution.py:71
  162.8 14.5 %fusion.24 = (f32[1024]{0:T(1024)S(1)}, f32[1024,768]{0,1:T(8,128)}) fusion(bf16[1024,5120]{0,1:T(8,128)(2,1)} %all-gather.5.cloned.1.call-done, bf16[5120,768]{1,0:T(8,128)(2,1)} %param.15), kind=kOutput, calls=%fused_computation.72 | convolution fusion | flops 8053849088 | bytes 21499904 | tf_op jit(solution)/shard_map/dot_general | solution.py:70
  177.3 68.4 %all-gather.3.cloned.1.call-done = bf16[1024,8192]{1,0:T(8,128)(2,1)} async-done(((bf16[1024,256]{1,0:T(8,128)(2,1)}), bf16[1024,8192]{1,0:T(8,128)(2,1)}) %all-gather.3.cloned.1.call-update) | async-done | bytes 16777232 | tf_op jit(solution)/shard_map/all_gather | solution.py:65
  245.7 20.5 %fusion.25 = (f32[1024]{0:T(1024)S(1)}, f32[1024,768]{0,1:T(8,128)}) fusion(bf16[1024,8192]{1,0:T(8,128)(2,1)} %all-gather.3.cloned.1.call-done, bf16[8192,768]{1,0:T(8,128)(2,1)} %param.14), kind=kOutput, calls=%fused_computation.73 | convolution fusion | flops 12885687296 | bytes 32509952 | tf_op jit(solution)/shard_map/dot_general | solution.py:64
  266.2 65.3 %all-reduce.1 = (f32[1024]{0:T(1024)S(1)}, f32[1024]{0:T(1024)S(1)}) all-reduce(f32[1024]{0:T(1024)S(1)} %get-tuple-element.32, f32[1024]{0:T(1024)S(1)} %get-tuple-element.30), channel_id=1, replica_groups=mesh['group'=2,'tok'=4,'vocab'=16] {'group','tok','vocab'}, use_global_device_ids=true, to_apply=%region_6.7 | all-reduce | flops 2048 | bytes 16384 | tf_op jit(solution)/shard_map/pmax | solution.py:86
  331.5 4.4 %select_reduce_fusion = (f32[1024]{0:T(1024)S(1)}, f32[1024]{0:T(1024)S(1)}, f32[1024]{0:T(1024)S(1)}, f32[1024]{0:T(1024)S(1)}) fusion(f32[1024,768]{0,1:T(8,128)} %get-tuple-element.31, s32[1024]{0:T(1024)S(1)} %select_subtract_fusion, f32[1024]{0:T(1024)S(1)} %get-tuple-element.30, f32[1024,768]{0,1:T(8,128)} %get-tuple-element.33, ...), kind=kLoop, calls=%fused_computation.6 | loop fusion | flops 7860224 | bytes 6320128 | tf_op jit(solution)/shard_map/reduce_sum | solution.py:85
  335.9 64.2 %all-reduce = (f32[1024]{0:T(1024)S(1)}, f32[1024]{0:T(1024)S(1)}, f32[1024]{0:T(1024)S(1)}, f32[1024]{0:T(1024)S(1)}) all-reduce(f32[1024]{0:T(1024)S(1)} %get-tuple-element.24, f32[1024]{0:T(1024)S(1)} %get-tuple-element.23, f32[1024]{0:T(1024)S(1)} %get-tuple-element.34, ...), channel_id=1, replica_groups=mesh['group'=2,'tok'=4,'vocab'=16] {'group','tok','vocab'}, use_global_device_ids=true, to_apply=%region_9.10 | all-reduce | flops 4096 | bytes 32768 | tf_op jit(solution)/shard_map/psum | solution.py:89
  400.1 0.7 select_reduce_fusion.2
  400.8 1.4 gather_fusion.5
  402.2 1.4 gather_fusion.2
  403.5 1.2 fusion.20
  404.8 1.2 fusion.21
  407.2 0.6 pad_maximum_fusion
  (13 shorter events, 0.1 us)
Async XLA Ops:
  7.2 16.6 %copy-start = (bf16[2048,256]{1,0:T(8,128)(2,1)S(1)}, bf16[2048,256]{1,0:T(8,128)(2,1)}, u32[]{:S(2)}) copy-start(bf16[2048,256]{1,0:T(8,128)(2,1)} %param.10) | copy-start | bytes 3145732
  7.2 155.6 %all-gather.5.cloned.1.call-start = ((), (), s32[]{:S(2)}) async-start(), calls=%async_computation.1 | async-start | bytes 10813440 | tf_op jit(solution)/shard_map/all_gather | solution.py:71
  8.1 95.5 %copy-start.4 = (bf16[160]{0:T(256)(128)(2,1)S(1)}, bf16[160]{0:T(256)(128)(2,1)}, u32[]{:S(2)}) copy-start(bf16[160]{0:T(256)(128)(2,1)} %param.13) | copy-start | bytes 964
  9.5 95.1 %copy-start.5 = (bf16[256]{0:T(256)(128)(2,1)S(1)}, bf16[256]{0:T(256)(128)(2,1)}, u32[]{:S(2)}) copy-start(bf16[256]{0:T(256)(128)(2,1)} %param.12) | copy-start | bytes 1540
  10.7 95.0 %copy-start.1 = (s32[1024]{0:T(1024)S(1)}, s32[1024]{0:T(1024)}, u32[]{:S(2)}) copy-start(s32[1024]{0:T(1024)} %param.17) | copy-start | bytes 12292
  104.5 6.5 %copy-start.3 = (s32[4]{0:T(128)S(1)}, s32[4]{0:T(128)}, u32[]{:S(2)}) copy-start(s32[4]{0:T(128)} %param.18) | copy-start | bytes 52
  104.5 7.9 %copy-start.2 = (s32[8192]{0:T(1024)S(1)}, s32[8192]{0:T(1024)}, u32[]{:S(2)}) copy-start(s32[8192]{0:T(1024)} %param.16) | copy-start | bytes 98308
  104.5 141.2 %all-gather.3.cloned.1.call-start = ((), (), s32[]{:S(2)}) async-start(), calls=%async_computation | async-start | bytes 17301504 | tf_op jit(solution)/shard_map/all_gather | solution.py:65
Sparse Core Ops, SparseCore 0:
  104.6 58.0 all-gather.4
  165.0 80.6 all-gather.2
where the time goes:
time: 416 us; the launch traced here: 415 us
  blocking collectives  221 us (53%)
  waiting for transfers between devices  109 us (26%)
  matrix products  35 us (8%)
  local copies, waits for them, and re-layouts  18.1 us (4%)
  between operations  16.9 us (4%)
  other arithmetic  14.4 us (3%)
    all_gather x1, waiting for transfers between devices, shards(): lax.all_gather(normed_teacher, ('group', 'vocab'), axis=1, tiled=True)  68.4 us
    psum x1, blocking collectives, shards(): lax.psum((jnp.sum(teacher_float * teacher_float, axis=1), jnp.sum(student...  65.6 us
    pmax x1, blocking collectives, shards(): lax.pmax((top_teacher, top_student), ('group', 'tok', 'vocab'))  65.3 us
    psum x1, blocking collectives, shards(): lax.psum((mass_teacher * shift_teacher, mass_student * shift_student, cro...  64.2 us
    all_gather x1, waiting for transfers between devices, shards(): lax.all_gather(normed_student, ('group', 'vocab'), axis=1, tiled=True)  41 us
    dot_general x1, matrix products, shards(): jnp.dot(lax.all_gather(normed_teacher, ('group', 'vocab'), axis=1, tiled=...  20.5 us
    dot_general x1, matrix products, shards(): jnp.dot(lax.all_gather(normed_student, ('group', 'vocab'), axis=1, tiled=...  14.5 us
    all_gather x1, blocking collectives, shards(): lax.all_gather(picked_student, 'tok', axis=0, tiled=True)  12.8 us
  transfers between devices with their start and end apart: 2, of which 2 were waited for; matrix products, arithmetic and copies ran while one was open for 7% of the time, Pallas kernels for 0%

commit v1 on v0

v1 whole, which is shorter than its diff:
```python
import functools

import jax
import jax.numpy as jnp
from jax import lax
from jax.experimental import pallas as pl
from jax.experimental.pallas import tpu as pltpu
from jax.sharding import PartitionSpec as P

EPS = 1e-06
MESH = pl.DeviceIdType.MESH
f32 = jnp.float32
bf16 = jnp.bfloat16

ROWS = 512
Q = 128
DT = 8192
DS = 5120
NV = 768
NT = 256
XT = 144

N_ICI = 24
N_SIB = 16


def off(i):
    return jnp.where(i < 2, i, 5 - i)


def body(
    th, sh, tg, sg, wt_hbm, ws_hbm, targets, positions, counts, mask_time,
    out_kl, out_nll, out_loss,
    ht, hs, wt, ws, xa, xb, xc, acc_t, acc_s, tok_col, tgt_col,
    pay, p1, tx, tz, ty, tgp, fx, fy, fz, fg,
    load_sem, p1_s, p1_r, rnd_s, rnd_r, ici_s, ici_r, sib_s, sib_r,
):
    g = lax.axis_index("group")
    x = lax.axis_index("tok")
    v = lax.axis_index("vocab")
    y = v // 4
    z = v % 4
    sib = {"group": 1 - g}

    def at_axis(axis, k):
        if axis == "x":
            return {"tok": (x + k) % 4}
        if axis == "y":
            return {"vocab": ((y + k) % 4) * 4 + z}
        return {"vocab": y * 4 + (z + k) % 4}

    loads = [
        pltpu.make_async_copy(th, ht, load_sem.at[0]),
        pltpu.make_async_copy(sh, hs, load_sem.at[1]),
    ]
    for i in range(4):
        r = pl.ds(i * (DT // 4), DT // 4)
        loads.append(pltpu.make_async_copy(wt_hbm.at[r], wt.at[r], load_sem.at[2 + i]))
        r = pl.ds(i * (DS // 4), DS // 4)
        loads.append(pltpu.make_async_copy(ws_hbm.at[r], ws.at[r], load_sem.at[6 + i]))
    for c in loads:
        c.start()

    barrier = pltpu.get_barrier_semaphore()
    peers = [at_axis(a, k) for a in "xyz" for k in (1, 2, 3)] + [sib]
    for d in peers:
        pl.semaphore_signal(barrier, inc=1, device_id=d, device_id_type=MESH)

    starts = []
    total = jnp.int32(0)
    for t in range(4):
        starts.append(total)
        total = total + counts[t]
    lane256 = lax.broadcasted_iota(jnp.int32, (1, 256), 1)
    pos_rows = []
    for t in range(4):
        p = jnp.concatenate([positions[2 * t : 2 * t + 1, :], positions[2 * t + 1 : 2 * t + 2, :]], axis=1)
        pos_rows.append(jnp.where(lane256 < counts[t], p + 2048 * t, 0))

    def tokens(q, _):
        d = (
            lax.broadcasted_iota(jnp.int32, (Q, 256), 0)
            + q * Q
            - lax.broadcasted_iota(jnp.int32, (Q, 256), 1)
        )
        s = jnp.zeros((Q, 256), jnp.int32)
        for t in range(4):
            s = s + jnp.where(d == starts[t], pos_rows[t], 0)
        tok_col[q] = jnp.sum(s.astype(f32), axis=1, keepdims=True)
        return 0

    lax.fori_loop(0, 4, tokens, 0)
    loads[0].wait()
    loads[1].wait()
    pl.semaphore_wait(barrier, len(peers))

    lane = lax.broadcasted_iota(jnp.int32, (Q, 128), 1)

    def tiny_copy(q, k):
        return pltpu.make_async_remote_copy(
            src_ref=tx.at[4 + q], dst_ref=tx.at[x], send_sem=rnd_s.at[0, k], recv_sem=rnd_r.at[0, k],
            device_id={"tok": q}, device_id_type=MESH)

    def pay_copy(q, k):
        return pltpu.make_async_remote_copy(
            src_ref=pay.at[q], dst_ref=p1.at[x], send_sem=p1_s.at[k], recv_sem=p1_r.at[k],
            device_id={"tok": q}, device_id_type=MESH)

    def pick(k, _):
        q = (x + 1 + jnp.where(k == 1, 2, jnp.where(k == 2, 1, k))) % 4
        tok = tok_col[q].astype(jnp.int32) - 2048 * x
        hot = jnp.where(tok == lax.broadcasted_iota(jnp.int32, (Q, 2048), 1), 1.0, 0.0).astype(bf16)
        ct = jnp.dot(hot, ht[...], preferred_element_type=f32)
        cs = jnp.dot(hot, hs[...], preferred_element_type=f32)
        sq_t = jnp.sum(ct * ct, axis=1, keepdims=True)
        sq_s = jnp.sum(cs * cs, axis=1, keepdims=True)
        rest = jnp.concatenate([cs[:, 128:160], jnp.zeros((Q, 96), f32)], axis=1)
        rest = jnp.where(lane == 32, sq_t, jnp.where(lane == 33, sq_s, rest))
        rest = jnp.transpose(rest)
        tx[4 + q] = rest[32:40]
        pay[q, 0:128] = ct[:, :128].astype(bf16)
        pay[q, 128:256] = ct[:, 128:].astype(bf16)
        pay[q, 256:384] = cs[:, :128].astype(bf16)
        pay[q, 384:416] = rest[:32].astype(bf16)

        @pl.when(k < 3)
        def _():
            tiny_copy(q, k).start()
            pay_copy(q, k).start()

        return 0

    lax.fori_loop(0, 4, pick, 0)

    for k in range(3):
        tiny_copy((x + 1) % 4, k).wait_recv()
    sums = tx[4 + x]
    for k in (1, 2, 3):
        sums = sums + tx[(x + k) % 4]

    def spread(buf, axis, at, number, rnd):
        if axis == "g":
            cps = [pltpu.make_async_remote_copy(
                src_ref=buf.at[at], dst_ref=buf.at[at], send_sem=rnd_s.at[rnd, 0], recv_sem=rnd_r.at[rnd, 0],
                device_id=sib, device_id_type=MESH)]
        else:
            cps = [pltpu.make_async_remote_copy(
                src_ref=buf.at[at], dst_ref=buf.at[at], send_sem=rnd_s.at[rnd, k - 1],
                recv_sem=rnd_r.at[rnd, k - 1], device_id=at_axis(axis, k), device_id_type=MESH)
                for k in (1, 3, 2)]
        for c in cps:
            c.start()
        for c in cps:
            c.wait_recv()
        ends.extend(cps)
        return [buf[i] for i in range(number)]

    ends = []
    for axis, buf, at, number, rnd in (("z", tz, z, 4, 1), ("y", ty, y, 4, 2), ("g", tgp, g, 2, 3)):
        buf[at] = sums
        parts = spread(buf, axis, at, number, rnd)
        sums = parts[0]
        for p in parts[1:]:
            sums = sums + p

    width = jnp.where(lax.broadcasted_iota(jnp.int32, (8, 128), 0) == 0, float(DT), float(DS))
    scale = lax.rsqrt(sums / width + EPS)
    scale_col = jnp.transpose(jnp.concatenate([scale, jnp.zeros((120, 128), f32)], axis=0))
    gain_t = tg[...].astype(f32)
    gain_s = sg[...].astype(f32)
    eye = lax.broadcasted_iota(jnp.int32, (32, 32), 0) == lax.broadcasted_iota(jnp.int32, (32, 32), 1)
    gain_col = jnp.sum(jnp.where(eye, gain_s[:, 128:160], 0.0), axis=1, keepdims=True)
    for k in range(3):
        pay_copy((x + 1) % 4, k).wait_recv()

    def mine(lo, hi):
        s = pay[x, lo:hi].astype(f32)
        for k in (1, 2, 3):
            s = s + p1[(x + k) % 4, lo:hi].astype(f32)
        return s

    xa[g, y, z, x, 0:128] = (mine(0, 128) * scale_col[:, 0:1] * gain_t[:, :128]).astype(bf16)
    xb[g, y, z, x, 0:128] = (mine(128, 256) * scale_col[:, 0:1] * gain_t[:, 128:]).astype(bf16)
    xc[g, y, z, x] = (mine(256, 384) * scale_col[:, 1:2] * gain_s[:, :128]).astype(bf16)
    rest = (mine(384, 416) * scale[1:2] * gain_col).astype(bf16)
    xa[g, y, z, x, 128:144] = rest[:16]
    xb[g, y, z, x, 128:144] = rest[16:]

    order = ("xyz", "yzx", "zxy")
    here = {"x": x, "y": y, "z": z}
    everything = slice(None)

    def box(c, a1, a2, a3):
        if c == 0:
            return xa.at[g, a2, a3, a1]
        if c == 1:
            return xb.at[g, a1, a2, a3]
        return xc.at[g, a3, a1, a2]

    def coords(c):
        return [here[a] for a in order[c]]

    def ici(c, n, ref, axis, k):
        return pltpu.make_async_remote_copy(
            src_ref=ref, dst_ref=ref, send_sem=ici_s.at[c, n], recv_sem=ici_r.at[c, n],
            device_id=at_axis(axis, k), device_id_type=MESH)

    def sibling(c, n, ref):
        return pltpu.make_async_remote_copy(
            src_ref=ref, dst_ref=ref, send_sem=sib_s.at[c, n], recv_sem=sib_r.at[c, n],
            device_id=sib, device_id_type=MESH)

    def first(c, n):
        a1, a2, a3 = coords(c)
        axis = order[c][0]
        cut = 64 if c == 2 else 80
        rows = 128 if c == 2 else XT
        if n == 0:
            return ici(c, 0, box(c, a1, a2, a3), axis, 1)
        if n == 1:
            return ici(c, 1, box(c, a1, a2, a3), axis, 3)
        if n == 2:
            return ici(c, 2, box(c, (a1 + 3) % 4, a2, a3).at[0:cut], axis, 1)
        return ici(c, 3, box(c, (a1 + 1) % 4, a2, a3).at[cut:rows], axis, 3)

    def second(c, n):
        a1, a2, a3 = coords(c)
        axis = order[c][1]
        if n == 0:
            return ici(c, 4, box(c, everything, a2, a3), axis, 1)
        if n == 1:
            return ici(c, 5, box(c, everything, a2, a3), axis, 3)
        if n == 2:
            return ici(c, 6, box(c, pl.ds(0, 2), (a2 + 3) % 4, a3), axis, 1)
        return ici(c, 7, box(c, pl.ds(2, 2), (a2 + 1) % 4, a3), axis, 3)

    def third(c, n, i):
        a1, a2, a3 = coords(c)
        axis = order[c][2]
        b2 = (a2 + off(i)) % 4
        if n == 0:
            return ici(c, 8 + i, box(c, everything, b2, a3), axis, 1)
        if n == 1:
            return ici(c, 12 + i, box(c, everything, b2, a3), axis, 3)
        if n == 2:
            return ici(c, 16 + i, box(c, pl.ds(0, 2), b2, (a3 + 3) % 4), axis, 1)
        return ici(c, 20 + i, box(c, pl.ds(2, 2), b2, (a3 + 1) % 4), axis, 3)

    def across(c, i, k):
        a1, a2, a3 = coords(c)
        return sibling(c, 4 * k + i, box(c, everything, (a2 + off(i)) % 4, (a3 + k) % 4))

    colors = range(3)
    for c in colors:
        first(c, 0).start()
        first(c, 1).start()

    digits = targets[...]
    table = jnp.concatenate(
        [(digits & 255), (digits >> 8) & 255, digits >> 16], axis=1).astype(f32).astype(bf16)
    first_entry = ((g * 4 + x) * 16 + v) * NV

    def find_targets(q, _):
        tok = tok_col[q].astype(jnp.int32)
        hot = jnp.where(
            (tok >> 7) == lax.broadcasted_iota(jnp.int32, (Q, 64), 1), 1.0, 0.0).astype(bf16)
        found = jnp.dot(hot, table, preferred_element_type=f32)
        mixed = found[:, :128] + 256.0 * found[:, 128:256] + 65536.0 * found[:, 256:]
        ids = jnp.sum(jnp.where(lane == (tok & 127), mixed, 0.0), axis=1, keepdims=True)
        tgt_col[q] = ids
        return 0

    lax.fori_loop(0, 4, find_targets, 0)
    acc_t[...] = jnp.zeros_like(acc_t)
    acc_s[...] = jnp.zeros_like(acc_s)

    for c in colors:
        first(c, 0).wait_recv()
        first(c, 2).start()
        first(c, 1).wait_recv()
        first(c, 3).start()
    for c in colors:
        first(c, 2).wait_recv()
        first(c, 3).wait_recv()
        second(c, 0).start()
        second(c, 1).start()
        third(c, 0, 0).start()
        third(c, 1, 0).start()
        across(c, 0, 0).start()
    for c in colors:
        second(c, 0).wait_recv()
        second(c, 2).start()
        second(c, 1).wait_recv()
        second(c, 3).start()
        for i in (1, 2):
            third(c, 0, i).start()
            third(c, 1, i).start()
            across(c, i, 0).start()
    for c in colors:
        second(c, 2).wait_recv()
        second(c, 3).wait_recv()
        third(c, 0, 3).start()
        third(c, 1, 3).start()
        across(c, 3, 0).start()
    for c in loads[2:]:
        c.wait()

    def add(acc, xs, w, rows_of):
        xs = jnp.concatenate(xs, axis=1)

        def one(n, _):
            cols = pl.ds(pl.multiple_of(n * NT, NT), NT)
            ws_ = jnp.concatenate([w[r, cols] for r in rows_of], axis=0)
            acc[:, cols] = acc[:, cols] + jnp.dot(xs, ws_, preferred_element_type=f32)
            return 0

        lax.fori_loop(0, NV // NT, one, 0)

    def chunk(gg, yy, zz):
        return gg * 16 + yy * 4 + zz

    def rows_t(n, odd):
        return pl.ds(pl.multiple_of(n * 256 + 128 * odd, 128), 128)

    def multiply(i, ks):
        y_i = (y + off(i)) % 4
        z_i = (z + off(i)) % 4
        x_i = (x + off(i)) % 4
        both = (0, 1)
        at = [(gg, y_i, (z + k) % 4) for k in ks for gg in both]
        add(acc_t, [xa[gg, yy, zz, :, 0:128].reshape(ROWS, 128) for gg, yy, zz in at],
            wt, [rows_t(chunk(*a), 0) for a in at])
        for k in ks:
            xx = (x + k) % 4
            at = [(gg, yy, z_i) for gg in both for yy in range(4)]
            add(acc_t.at[pl.ds(pl.multiple_of(xx * Q, Q), Q)],
                [xb[gg, yy, zz, xx, 0:128] for gg, yy, zz in at],
                wt, [rows_t(chunk(*a), 1) for a in at])
        at = [(gg, (y + k) % 4, zz) for k in ks for gg in both for zz in range(4)]
        add(acc_s.at[pl.ds(pl.multiple_of(x_i * Q, Q), Q)],
            [xc[gg, yy, zz, x_i] for gg, yy, zz in at],
            ws, [pl.ds(pl.multiple_of(chunk(*a) * 160, 32), 128) for a in at])

    def multiply_rest(i):
        y_i = (y + off(i)) % 4
        z_i = (z + off(i)) % 4
        both = (0, 1)
        at_a = [(gg, y_i, zz) for gg in both for zz in range(4)]
        at_b = [(gg, yy, z_i) for gg in both for yy in range(4)]
        xs = []
        for xx in range(4):
            t = jnp.concatenate(
                [xa[gg, yy, zz, xx, 128:144] for gg, yy, zz in at_a]
                + [xb[gg, yy, zz, xx, 128:144] for gg, yy, zz in at_b], axis=0)
            xs.append(jnp.transpose(t.astype(f32)).astype(bf16))
        rows_of = [pl.ds(pl.multiple_of(chunk(*a) * 160 + 128, 16), 16) for a in at_a]
        rows_of += [pl.ds(pl.multiple_of(chunk(*a) * 160 + 144, 16), 16) for a in at_b]
        add(acc_s, [jnp.concatenate(xs, axis=0)], ws, rows_of)

    def step(i, _):
        for c in colors:
            third(c, 0, i).wait_recv()
            third(c, 2, i).start()
            across(c, i, 3).start()
            third(c, 1, i).wait_recv()
            third(c, 3, i).start()
            across(c, i, 1).start()
        for c in colors:
            for k in (0, 1, 3):
                across(c, i, k).wait_recv()
        multiply(i, (0, 1, 3))
        for c in colors:
            third(c, 2, i).wait_recv()
            third(c, 3, i).wait_recv()
            across(c, i, 2).start()
        for c in colors:
            across(c, i, 2).wait_recv()
        multiply(i, (2,))
        multiply_rest(i)
        return 0

    lax.fori_loop(0, 4, step, 0)

    def stats(q, m):
        r = pl.ds(pl.multiple_of(q * Q, Q), Q)
        lt = acc_t[r, :]
        ls = acc_s[r, :]
        mt = jnp.max(lt, axis=1, keepdims=True)
        ms = jnp.max(ls, axis=1, keepdims=True)
        et = jnp.exp(lt - mt)
        zt = jnp.sum(et, axis=1, keepdims=True)
        dd = jnp.sum(et * (lt - ls), axis=1, keepdims=True)
        zs = jnp.sum(jnp.exp(ls - ms), axis=1, keepdims=True)
        col = tgt_col[q].astype(jnp.int32) - first_entry
        hit = col == lax.broadcasted_iota(jnp.int32, (Q, NV), 1)
        tl = jnp.sum(jnp.where(hit, ls, 0.0), axis=1, keepdims=True)
        for n, val in enumerate((mt + jnp.log(zt), ms + jnp.log(zs), dd / zt, tl)):
            m = jnp.where(lane == 4 * n + q, val, m)
        return m

    m = lax.fori_loop(0, 4, stats, jnp.zeros((Q, 128), f32))
    val = jnp.transpose(m)[:16]

    for axis, buf, at, number, rnd in (("g", fg, g, 2, 4), ("x", fx, x, 4, 5), ("y", fy, y, 4, 6), ("z", fz, z, 4, 7)):
        buf[at] = val
        parts = spread(buf, axis, at, number, rnd)

        def lse(lo):
            top = parts[0][lo : lo + 4]
            for p in parts[1:]:
                top = jnp.maximum(top, p[lo : lo + 4])
            es = [jnp.exp(p[lo : lo + 4] - top) for p in parts]
            tot = es[0]
            for e in es[1:]:
                tot = tot + e
            return top + jnp.log(tot), es, tot

        lse_t, es, tot = lse(0)
        lse_s, _, _ = lse(4)
        cross = es[0] * parts[0][8:12]
        tl = parts[0][12:16]
        for e, p in zip(es[1:], parts[1:]):
            cross = cross + e * p[8:12]
            tl = tl + p[12:16]
        val = jnp.concatenate([lse_t, lse_s, cross / tot, tl], axis=0)

    lse_t, lse_s, cross, tl = (val[4 * n : 4 * n + 4] for n in range(4))
    kl = cross - lse_t + lse_s
    nll = lse_s - tl
    kl_total = jnp.sum(jnp.sum(kl, axis=1, keepdims=True), axis=0, keepdims=True)
    nll_total = jnp.sum(jnp.sum(nll, axis=1, keepdims=True), axis=0, keepdims=True)
    time = jnp.full((1, 1), mask_time[0], jnp.int32).astype(f32)
    masked = jnp.full((1, 1), total, jnp.int32).astype(f32)
    weight = 1000.0 / time
    out_loss[...] = jnp.concatenate([weight * nll_total / 8192.0, kl_total / masked], axis=1)

    cols = jnp.transpose(jnp.concatenate([kl, nll, jnp.zeros((120, 128), f32)], axis=0))
    start = jnp.int32(0)
    count = jnp.int32(0)
    for t in range(4):
        start = start + jnp.where(x == t, starts[t], 0)
        count = count + jnp.where(x == t, counts[t], 0)
    slot = lax.broadcasted_iota(jnp.int32, (Q, 256), 1)
    gap = lax.broadcasted_iota(jnp.int32, (Q, 256), 0) - slot
    for n, out in ((0, out_kl), (4, out_nll)):
        s = jnp.zeros((Q, 256), f32)
        for q in range(4):
            s = s + jnp.where(gap == start - q * Q, cols[:, n + q : n + q + 1], 0.0)
        s = jnp.sum(s, axis=0, keepdims=True)
        out[...] = jnp.where(lane256 < count, s, 0.0)

    for k in range(3):
        tiny_copy((x + 1) % 4, k).wait_send()
        pay_copy((x + 1) % 4, k).wait_send()
    for c in ends:
        c.wait_send()
    for c in colors:
        for n in range(4):
            first(c, n).wait_send()
            second(c, n).wait_send()

    def drain(i, _):
        for c in colors:
            for n in range(4):
                third(c, n, i).wait_send()
                across(c, i, n).wait_send()
        return 0

    lax.fori_loop(0, 4, drain, 0)


def shards(th, sh, tg, sg, wt, ws, targets, positions, counts, mask_time):
    vm = pl.BlockSpec(memory_space=pltpu.VMEM)
    sm = pl.BlockSpec(memory_space=pltpu.SMEM)
    anyspace = pl.BlockSpec(memory_space=pl.ANY)
    dma = pltpu.SemaphoreType.DMA
    kl, nll, loss = pl.pallas_call(
        body,
        out_shape=(
            jax.ShapeDtypeStruct((1, 256), f32),
            jax.ShapeDtypeStruct((1, 256), f32),
            jax.ShapeDtypeStruct((1, 2), f32),
        ),
        in_specs=[anyspace, anyspace, vm, vm, anyspace, anyspace, vm, vm, sm, sm],
        out_specs=(vm, vm, vm),
        scratch_shapes=[
            pltpu.VMEM((2048, 256), bf16),
            pltpu.VMEM((2048, 160), bf16),
            pltpu.VMEM((DT, NV), bf16),
            pltpu.VMEM((DS, NV), bf16),
            pltpu.VMEM((2, 4, 4, 4, XT, 128), bf16),
            pltpu.VMEM((2, 4, 4, 4, XT, 128), bf16),
            pltpu.VMEM((2, 4, 4, 4, 128, 128), bf16),
            pltpu.VMEM((ROWS, NV), f32),
            pltpu.VMEM((ROWS, NV), f32),
            pltpu.VMEM((4, Q, 1), f32),
            pltpu.VMEM((4, Q, 1), f32),
            pltpu.VMEM((4, 416, 128), bf16),
            pltpu.VMEM((4, 416, 128), bf16),
            pltpu.VMEM((8, 8, 128), f32),
            pltpu.VMEM((4, 8, 128), f32),
            pltpu.VMEM((4, 8, 128), f32),
            pltpu.VMEM((2, 8, 128), f32),
            pltpu.VMEM((4, 16, 128), f32),
            pltpu.VMEM((4, 16, 128), f32),
            pltpu.VMEM((4, 16, 128), f32),
            pltpu.VMEM((2, 16, 128), f32),
            dma((10,)),
            dma((3,)),
            dma((3,)),
            dma((8, 3)),
            dma((8, 3)),
            dma((3, N_ICI)),
            dma((3, N_ICI)),
            dma((3, N_SIB)),
            dma((3, N_SIB)),
        ],
        compiler_params=pltpu.CompilerParams(
            collective_id=0, has_side_effects=True, vmem_limit_bytes=58 * 1024 * 1024),
        name="elbo",
    )(
        th, sh, tg.reshape(1, 256), sg.reshape(1, 160), wt, ws,
        targets.reshape(64, 128), positions.reshape(8, 128), counts, mask_time,
    )
    return kl.reshape(256), nll.reshape(256), loss.reshape(2)


def solution(mesh):
    feats = ("group", "vocab")
    cols = ("group", "tok", "vocab")
    in_specs = (
        P("tok", feats), P("tok", feats), P(feats), P(feats),
        P(None, cols), P(None, cols), P(), P(), P(), P(),
    )
    out_specs = (P("tok"), P("tok"), P())
    return jax.shard_map(shards, mesh=mesh, in_specs=in_specs, out_specs=out_specs, check_vma=False)
```

time: 416 us -> 116 us (0.28)
  blocking collectives: 221 us -> 0 us
  waiting for transfers between devices: 109 us -> 0 us
  Pallas kernels: 0 us -> 106 us
  matrix products: 35 us -> 0 us
  between operations: 16.9 us -> 1.29 us
  other arithmetic: 14.4 us -> 0 us
  local copies, waits for them, and re-layouts: 18.1 us -> 8.28 us
    psum x2 -> x0, blocking collectives: 130 us -> none  [the longest x1 65.6 us: shards(): lax.psum((jnp.sum(teacher_float * teacher_float, axis=1), jnp.sum(student...]
    all_gather x2 -> x0, waiting for transfers between devices: 109 us -> none  [the longest x1 68.4 us: shards(): lax.all_gather(normed_teacher, ('group', 'vocab'), axis=1, tiled=True)]
    pallas_call x0 -> x1, Pallas kernels: none -> 106 us  [shards(): pl.pallas_call(body, out_shape=(jax.ShapeDtypeStruct((1, 256), f32), jax....]
    pmax x1 -> x0, blocking collectives: 65.3 us -> none  [shards(): lax.pmax((top_teacher, top_student), ('group', 'tok', 'vocab'))]
    dot_general x2 -> x0, matrix products: 35 us -> none  [the longest x1 20.5 us: shards(): jnp.dot(lax.all_gather(normed_teacher, ('group', 'vocab'), axis=1, tiled=...]
    all_gather x2 -> x0, blocking collectives: 25.6 us -> none  [the longest x1 12.8 us: shards(): lax.all_gather(picked_student, 'tok', axis=0, tiled=True)]
    gather x7 -> x0, local copies, waits for them, and re-layouts: 16 us -> none  [the longest x1 6.15 us: shards(): target_ids = jnp.take(targets, token_index)]
    reduce_sum x5 -> x0, other arithmetic: 6.05 us -> none  [the longest x1 4.43 us: shards(): target_logit = jnp.sum(jnp.where(target_hit, logit_student, 0.0), axis=1)]
  transfers between devices with their start and end apart: 2 -> 0, of which waited for: 2 -> 0; matrix products, arithmetic and copies ran while one was open for 7% -> 0% of each run, Pallas kernels for 0% -> 0%
where the time goes in v1:
time: 116 us
  Pallas kernels  106 us (91%)
  local copies, waits for them, and re-layouts  8.28 us (7%)
  between operations  1.29 us (1%)
    pallas_call x1, Pallas kernels, shards(): pl.pallas_call(body, out_shape=(jax.ShapeDtypeStruct((1, 256), f32), jax....  106 us
    unnamed x4, local copies, waits for them, and re-layouts  5.84 us

profile of v1, /device:TPU:0, one launch (start us, length us, event | category | flops | bytes accessed | tf_op | source)
XLA Modules:
  0.0 116.1 jit_solution(6362468235293544373)
XLA Ops:
  1.3 1.2 %reshape.27.tg = bf16[1,256]{1,0:T(2,128)(2,1)} reshape(bf16[256]{0:T(256)(128)(2,1)} %param.12) | data formatting | bytes 1024 | tf_op jit(solution)/shard_map/reshape | solution.py:522
  2.5 1.2 %reshape.28.sg = bf16[1,160]{1,0:T(2,128)(2,1)} reshape(bf16[160]{0:T(256)(128)(2,1)} %param.13) | data formatting | bytes 640 | tf_op jit(solution)/shard_map/reshape | solution.py:522
  3.7 2.2 %copy.13.sh = bf16[2048,160]{1,0:T(8,128)(2,1)} copy(bf16[2048,160]{0,1:T(8,128)(2,1)} %param.11) | data formatting | bytes 1310720 | tf_op args[1]
  5.9 106.5 %elbo.1 = (f32[1,256]{1,0:T(1,128)}, f32[1,256]{1,0:T(1,128)}, f32[1,2]{1,0:T(1,128)}) custom-call(bf16[2048,256]{1,0:T(8,128)(2,1)} %th.1, bf16[2048,160]{1,0:T(8,128)(2,1)} %copy.13.sh, bf16[1,256]{1,0:T(2,128)(2,1)} %reshape.27.tg, bf16[1,160]{1,0:T(2,128)(2,1)} %reshape.28.sg, bf16[8192,768]{1,0:T(8,128)(2,1)} %wt_hbm.1, bf16[5120,768]{1,0:T(8,128)(2,1)} %ws_hbm.1, ...), custom_call_target="tpu_custom_call" | custom-call | tf_op jit(solution)/shard_map/elbo/pallas_call | solution.py:477
  112.4 1.2 %copy.18 = f32[256]{0:T(256)} copy(f32[256]{0:T(256)} %bitcast.8) | data formatting | bytes 2048
  113.7 1.2 %copy.19 = f32[256]{0:T(256)} copy(f32[256]{0:T(256)} %bitcast.7) | data formatting | bytes 2048
  114.9 1.2 %copy.20 = f32[2]{0:T(128)} copy(f32[2]{0:T(128)} %bitcast.9) | data formatting | bytes 16

commit v2 on v1

v2 whole, which is shorter than its diff:
```python
import functools

import jax
import jax.numpy as jnp
from jax import lax
from jax.experimental import pallas as pl
from jax.experimental.pallas import tpu as pltpu
from jax.sharding import PartitionSpec as P

EPS = 1e-06
MESH = pl.DeviceIdType.MESH
f32 = jnp.float32
bf16 = jnp.bfloat16

ROWS = 512
Q = 128
DT = 8192
DS = 5120
NV = 768
NT = 256
XT = 144

N_ICI = 24
N_SIB = 16


def off(i):
    return jnp.where(i < 2, i, 5 - i)


def body(
    th, sh, tg_any, sg, wt_hbm, ws_hbm, targets_any, positions_any, counts,
    out,
    ht, hs, tg, targets, positions, hot, wt, ws, xa, xb, xc, acc_t, acc_s, tok_col, tgt_col,
    sc_t, sc_s, pay_a, pay_b, pay_c, p1a, p1b, p1c, tx, tz, ty, tgp, txx, fx, fy, fz,
    load_sem, p1_s, p1_r, rnd_s, rnd_r, ici_s, ici_r, sib_s, sib_r,
):
    g = lax.axis_index("group")
    x = lax.axis_index("tok")
    v = lax.axis_index("vocab")
    y = v // 4
    z = v % 4
    sib = {"group": 1 - g}

    def at_axis(axis, k):
        if axis == "x":
            return {"tok": (x + k) % 4}
        if axis == "y":
            return {"vocab": ((y + k) % 4) * 4 + z}
        return {"vocab": y * 4 + (z + k) % 4}

    barrier = pltpu.get_barrier_semaphore()
    peers = [at_axis(a, k) for a in "xyz" for k in (1, 2, 3)] + [sib]
    peers += [{"group": 1 - g, "tok": (x + k) % 4} for k in (1, 2, 3)]
    for d in peers:
        pl.semaphore_signal(barrier, inc=1, device_id=d, device_id_type=MESH)

    small = [
        pltpu.make_async_copy(positions_any, positions, load_sem.at[10]),
        pltpu.make_async_copy(tg_any, tg, load_sem.at[11]),
        pltpu.make_async_copy(targets_any, targets, load_sem.at[12]),
    ]
    loads = [
        pltpu.make_async_copy(th, ht, load_sem.at[0]),
        pltpu.make_async_copy(sh, hs, load_sem.at[1]),
    ]
    for i in range(4):
        r = pl.ds(i * (DT // 4), DT // 4)
        loads.append(pltpu.make_async_copy(wt_hbm.at[r], wt.at[r], load_sem.at[2 + i]))
        r = pl.ds(i * (DS // 4), DS // 4)
        loads.append(pltpu.make_async_copy(ws_hbm.at[r], ws.at[r], load_sem.at[6 + i]))
    for c in small + loads:
        c.start()

    starts = []
    total = jnp.int32(0)
    for t in range(4):
        starts.append(total)
        total = total + counts[t]
    lane256 = lax.broadcasted_iota(jnp.int32, (1, 256), 1)
    small[0].wait()
    pos_rows = []
    for t in range(4):
        p = jnp.concatenate([positions[2 * t : 2 * t + 1, :], positions[2 * t + 1 : 2 * t + 2, :]], axis=1)
        pos_rows.append(jnp.where(lane256 < counts[t], p + 2048 * t, 0))

    def tokens(q, _):
        d = (
            lax.broadcasted_iota(jnp.int32, (Q, 256), 0)
            + q * Q
            - lax.broadcasted_iota(jnp.int32, (Q, 256), 1)
        )
        s = jnp.zeros((Q, 256), jnp.int32)
        for t in range(4):
            s = s + jnp.where(d == starts[t], pos_rows[t], 0)
        tok_col[q] = jnp.sum(s.astype(f32), axis=1, keepdims=True)
        return 0

    lax.fori_loop(0, 4, tokens, 0)

    lane = lax.broadcasted_iota(jnp.int32, (Q, 128), 1)

    def tiny_copy(q, k):
        return pltpu.make_async_remote_copy(
            src_ref=tx.at[4 + q], dst_ref=tx.at[x], send_sem=rnd_s.at[0, k], recv_sem=rnd_r.at[0, k],
            device_id={"tok": q}, device_id_type=MESH)

    pays = ((pay_a, p1a), (pay_b, p1b), (pay_c, p1c))

    def pay_copy(c, q, k):
        src, dst = pays[c]
        return pltpu.make_async_remote_copy(
            src_ref=src.at[q], dst_ref=dst.at[x], send_sem=p1_s.at[c, k], recv_sem=p1_r.at[c, k],
            device_id={"tok": q}, device_id_type=MESH)

    def to(k):
        return (x + 1 + jnp.where(k == 1, 2, jnp.where(k == 2, 1, k))) % 4

    def make_hot(q, _):
        tok = tok_col[q].astype(jnp.int32) - 2048 * x
        hot[pl.ds(pl.multiple_of(q * Q, Q), Q), :] = jnp.where(
            tok == lax.broadcasted_iota(jnp.int32, (Q, 2048), 1), 1.0, 0.0).astype(bf16)
        return 0

    lax.fori_loop(0, 4, make_hot, 0)
    loads[0].wait()
    ct = jnp.dot(hot[...], ht[...], preferred_element_type=f32)
    for q in range(4):
        cq = ct[q * Q : (q + 1) * Q]
        sc_t[q] = jnp.sum(cq * cq, axis=1, keepdims=True)
        pay_a[q] = cq[:, :128].astype(bf16)
        pay_b[q] = cq[:, 128:].astype(bf16)
    pl.semaphore_wait(barrier, len(peers))
    for k in range(3):
        pay_copy(1, to(k), k).start()
    loads[1].wait()
    cs = lax.dot_general(hot[...], hs[...], (((1,), (1,)), ((), ())), preferred_element_type=f32)
    for q in range(4):
        cq = cs[q * Q : (q + 1) * Q]
        sq_s = jnp.sum(cq * cq, axis=1, keepdims=True)
        rest = jnp.concatenate([cq[:, 128:160], jnp.zeros((Q, 96), f32)], axis=1)
        rest = jnp.where(lane == 32, sc_t[q], jnp.where(lane == 33, sq_s, rest))
        rest = jnp.transpose(rest)
        tx[4 + q] = rest[32:40]
        pay_c[q, 0:128] = cq[:, :128].astype(bf16)
        pay_c[q, 128:160] = rest[:32].astype(bf16)
    for k in range(3):
        pay_copy(2, to(k), k).start()
    for k in range(3):
        tiny_copy(to(k), k).start()
    for k in range(3):
        pay_copy(0, to(k), k).start()

    ends = []

    def spread(buf, axis, at, number, rnd, value):
        buf[at] = value
        if axis == "gx":
            devs = [sib] + [at_axis("x", k) for k in (1, 3, 2)]
            devs += [{"group": 1 - g, "tok": (x + k) % 4} for k in (1, 3, 2)]
            cps = [pltpu.make_async_remote_copy(
                src_ref=buf.at[at], dst_ref=buf.at[at], send_sem=rnd_s.at[rnd, n], recv_sem=rnd_r.at[rnd, n],
                device_id=d, device_id_type=MESH) for n, d in enumerate(devs)]
        elif axis == "g":
            cps = [pltpu.make_async_remote_copy(
                src_ref=buf.at[at], dst_ref=buf.at[at], send_sem=rnd_s.at[rnd, 0], recv_sem=rnd_r.at[rnd, 0],
                device_id=sib, device_id_type=MESH)]
        else:
            cps = [pltpu.make_async_remote_copy(
                src_ref=buf.at[at], dst_ref=buf.at[at], send_sem=rnd_s.at[rnd, k - 1],
                recv_sem=rnd_r.at[rnd, k - 1], device_id=at_axis(axis, k), device_id_type=MESH)
                for k in (1, 3, 2)]
        for c in cps:
            c.start()
        ends.extend(cps)

        def finish():
            for c in cps:
                c.wait_recv()
            return [buf[i] for i in range(number)]

        return finish

    def add_up(parts):
        total = parts[0]
        for p in parts[1:]:
            total = total + p
        return total

    def sums_x():
        for k in range(3):
            tiny_copy((x + 1) % 4, k).wait_recv()
        return add_up([tx[4 + x]] + [tx[(x + k) % 4] for k in (1, 2, 3)])

    small[1].wait()
    gain_t = tg[...].astype(f32)
    gain_s = sg[...].astype(f32).reshape(1, 160)
    eye = lax.broadcasted_iota(jnp.int32, (32, 32), 0) == lax.broadcasted_iota(jnp.int32, (32, 32), 1)
    gain_col = jnp.sum(jnp.where(eye, gain_s[:, 128:160], 0.0), axis=1, keepdims=True)

    def mine(c, lo, hi):
        own, others = pays[c]
        s = own[x, lo:hi].astype(f32)
        for k in (1, 2, 3):
            s = s + others[(x + k) % 4, lo:hi].astype(f32)
        return s

    def place(c):
        for k in range(3):
            pay_copy(c, to(k), k).wait_recv()
        if c == 0:
            xa[g, y, z, x, 0:128] = (mine(0, 0, 128) * gain_t[0:1]).astype(bf16)
        elif c == 1:
            xb[g, y, z, x] = (mine(1, 0, 128) * gain_t[1:2]).astype(bf16)
        else:
            xc[g, y, z, x, 0:128] = (mine(2, 0, 128) * gain_s[:, :128]).astype(bf16)
            rest = (mine(2, 128, 160) * gain_col).astype(bf16)
            xa[g, y, z, x, 128:144] = rest[:16]
            xc[g, y, z, x, 128:144] = rest[16:]

    order = ("xyz", "yzx", "zxy")
    here = {"x": x, "y": y, "z": z}
    everything = slice(None)

    def box(c, a1, a2, a3):
        if c == 0:
            return xa.at[g, a2, a3, a1]
        if c == 1:
            return xb.at[g, a1, a2, a3]
        return xc.at[g, a3, a1, a2]

    def coords(c):
        return [here[a] for a in order[c]]

    def ici(c, n, ref, axis, k):
        return pltpu.make_async_remote_copy(
            src_ref=ref, dst_ref=ref, send_sem=ici_s.at[c, n], recv_sem=ici_r.at[c, n],
            device_id=at_axis(axis, k), device_id_type=MESH)

    def sibling(c, n, ref):
        return pltpu.make_async_remote_copy(
            src_ref=ref, dst_ref=ref, send_sem=sib_s.at[c, n], recv_sem=sib_r.at[c, n],
            device_id=sib, device_id_type=MESH)

    def first(c, n):
        return ici(c, n, box(c, *coords(c)), order[c][0], (1, 3, 2)[n])

    def second(c, n):
        a1, a2, a3 = coords(c)
        axis = order[c][1]
        if n == 0:
            return ici(c, 4, box(c, everything, a2, a3), axis, 1)
        if n == 1:
            return ici(c, 5, box(c, everything, a2, a3), axis, 3)
        if n == 2:
            return ici(c, 6, box(c, pl.ds(0, 2), (a2 + 3) % 4, a3), axis, 1)
        return ici(c, 7, box(c, pl.ds(2, 2), (a2 + 1) % 4, a3), axis, 3)

    def third(c, n, i):
        a1, a2, a3 = coords(c)
        axis = order[c][2]
        b2 = (a2 + off(i)) % 4
        if n == 0:
            return ici(c, 8 + i, box(c, everything, b2, a3), axis, 1)
        if n == 1:
            return ici(c, 12 + i, box(c, everything, b2, a3), axis, 3)
        if n == 2:
            return ici(c, 16 + i, box(c, pl.ds(0, 2), b2, (a3 + 3) % 4), axis, 1)
        return ici(c, 20 + i, box(c, pl.ds(2, 2), b2, (a3 + 1) % 4), axis, 3)

    def across(c, i, k):
        a1, a2, a3 = coords(c)
        return sibling(c, 4 * k + i, box(c, everything, (a2 + off(i)) % 4, (a3 + k) % 4))

    colors = (1, 2, 0)
    for c in colors:
        place(c)
        for n in range(3):
            first(c, n).start()
    finish = spread(tz, "z", z, 4, 1, sums_x())

    small[2].wait()
    digits = targets[...]
    table = jnp.concatenate(
        [(digits & 255), (digits >> 8) & 255, digits >> 16], axis=1).astype(f32).astype(bf16)
    first_entry = ((g * 4 + x) * 16 + v) * NV

    def find_targets(q, _):
        tok = tok_col[q].astype(jnp.int32)
        hot = jnp.where(
            (tok >> 7) == lax.broadcasted_iota(jnp.int32, (Q, 64), 1), 1.0, 0.0).astype(bf16)
        found = jnp.dot(hot, table, preferred_element_type=f32)
        mixed = found[:, :128] + 256.0 * found[:, 128:256] + 65536.0 * found[:, 256:]
        ids = jnp.sum(jnp.where(lane == (tok & 127), mixed, 0.0), axis=1, keepdims=True)
        tgt_col[q] = ids
        return 0

    lax.fori_loop(0, 4, find_targets, 0)
    acc_t[...] = jnp.zeros_like(acc_t)
    acc_s[...] = jnp.zeros_like(acc_s)

    for c in colors:
        for n in range(3):
            first(c, n).wait_recv()
        second(c, 0).start()
        second(c, 1).start()
    for c in colors:
        third(c, 0, 0).start()
        third(c, 1, 0).start()
        across(c, 0, 0).start()
    finish = spread(ty, "y", y, 4, 2, add_up(finish()))
    for c in colors:
        second(c, 0).wait_recv()
        second(c, 2).start()
        second(c, 1).wait_recv()
        second(c, 3).start()
    for c in colors:
        for i in (1, 2):
            third(c, 0, i).start()
            third(c, 1, i).start()
            across(c, i, 0).start()
    finish = spread(tgp, "g", g, 2, 3, add_up(finish()))
    for c in loads[2:]:
        c.wait()
    for c in colors:
        second(c, 2).wait_recv()
        second(c, 3).wait_recv()
        third(c, 0, 3).start()
        third(c, 1, 3).start()
        across(c, 3, 0).start()
    finish = spread(txx, "x", x, 4, 8, add_up(finish()))

    def add(acc, xs, w, rows_of):
        xs = jnp.concatenate(xs, axis=1)

        ws_ = jnp.concatenate([w[r, :] for r in rows_of], axis=0)
        acc[...] = acc[...] + jnp.dot(xs, ws_, preferred_element_type=f32)

    def chunk(gg, yy, zz):
        return gg * 16 + yy * 4 + zz

    def rows_t(n, odd):
        return pl.ds(pl.multiple_of(n * 256 + 128 * odd, 128), 128)

    def multiply(i, ks):
        y_i = (y + off(i)) % 4
        z_i = (z + off(i)) % 4
        x_i = (x + off(i)) % 4
        both = (0, 1)
        at = [(gg, y_i, (z + k) % 4) for k in ks for gg in both]
        add(acc_t, [xa[gg, yy, zz, :, 0:128].reshape(ROWS, 128) for gg, yy, zz in at],
            wt, [rows_t(chunk(*a), 0) for a in at])
        for k in ks:
            xx = (x + k) % 4
            at = [(gg, yy, z_i) for gg in both for yy in range(4)]
            add(acc_t.at[pl.ds(pl.multiple_of(xx * Q, Q), Q)],
                [xb[gg, yy, zz, xx] for gg, yy, zz in at],
                wt, [rows_t(chunk(*a), 1) for a in at])
        at = [(gg, (y + k) % 4, zz) for k in ks for gg in both for zz in range(4)]
        add(acc_s.at[pl.ds(pl.multiple_of(x_i * Q, Q), Q)],
            [xc[gg, yy, zz, x_i, 0:128] for gg, yy, zz in at],
            ws, [pl.ds(pl.multiple_of(chunk(*a) * 160, 32), 128) for a in at])

    def multiply_rest(i):
        y_i = (y + off(i)) % 4
        x_i = (x + off(i)) % 4
        at = [(gg, y_i, zz) for gg in (0, 1) for zz in range(4)]
        xs = []
        for xx in range(4):
            t = jnp.concatenate([xa[gg, yy, zz, xx, 128:144] for gg, yy, zz in at], axis=0)
            xs.append(jnp.transpose(t.astype(f32)).astype(bf16))
        add(acc_s, [jnp.concatenate(xs, axis=0)], ws,
            [pl.ds(pl.multiple_of(chunk(*a) * 160 + 128, 16), 16) for a in at])
        xs = []
        rows_of = []
        for gg in (0, 1):
            for yp in (0, 2):
                at = [(gg, yy, zz) for yy in (yp, yp + 1) for zz in range(4)]
                t = jnp.concatenate([xc[gg, yy, zz, x_i, 128:144] for gg, yy, zz in at], axis=0)
                xs.append(jnp.transpose(t.astype(f32)).astype(bf16))
                rows_of += [pl.ds(pl.multiple_of(chunk(*a) * 160 + 144, 16), 16) for a in at]
        add(acc_s.at[pl.ds(pl.multiple_of(x_i * Q, Q), Q)], xs, ws, rows_of)

    def step(i, _):
        def opposite(j):
            for c in colors:
                third(c, 2, j).wait_recv()
                third(c, 3, j).wait_recv()
                across(c, j, 2).start()

        @pl.when(i < 4)
        def _():
            for c in colors:
                third(c, 0, i).wait_recv()
                third(c, 2, i).start()
                third(c, 1, i).wait_recv()
                third(c, 3, i).start()
                across(c, i, 3).start()
                across(c, i, 1).start()
            for c in colors:
                across(c, i, 0).wait_recv()
            multiply(i, (0,))

        @pl.when((i > 0) & (i < 4))
        def _():
            opposite(i - 1)

        @pl.when((i > 0) & (i < 5))
        def _():
            for c in colors:
                for k in (1, 3):
                    across(c, i - 1, k).wait_recv()
            multiply(i - 1, (1, 3))

        @pl.when(i > 1)
        def _():
            for c in colors:
                across(c, i - 2, 2).wait_recv()
            multiply(i - 2, (2,))
            multiply_rest(i - 2)

        @pl.when(i == 4)
        def _():
            opposite(3)

        return 0

    lax.fori_loop(0, 6, step, 0)

    parts = finish()
    width = jnp.where(lax.broadcasted_iota(jnp.int32, (8, 128), 0) % 2 == 0, float(DT), float(DS))
    scale = lax.rsqrt(jnp.concatenate([p[0:2] for p in parts], axis=0) / width + EPS)
    scale = jnp.transpose(jnp.concatenate([scale, jnp.zeros((120, 128), f32)], axis=0))
    for q in range(4):
        sc_t[q] = scale[:, 2 * q : 2 * q + 1]
        sc_s[q] = scale[:, 2 * q + 1 : 2 * q + 2]

    def stats(q, m):
        r = pl.ds(pl.multiple_of(q * Q, Q), Q)
        lt = acc_t[r, :] * sc_t[q]
        ls = acc_s[r, :] * sc_s[q]
        mt = jnp.max(lt, axis=1, keepdims=True)
        ms = jnp.max(ls, axis=1, keepdims=True)
        et = jnp.exp(lt - mt)
        zt = jnp.sum(et, axis=1, keepdims=True)
        dd = jnp.sum(et * (lt - ls), axis=1, keepdims=True)
        zs = jnp.sum(jnp.exp(ls - ms), axis=1, keepdims=True)
        col = tgt_col[q].astype(jnp.int32) - first_entry
        hit = col == lax.broadcasted_iota(jnp.int32, (Q, NV), 1)
        tl = jnp.sum(jnp.where(hit, ls, 0.0), axis=1, keepdims=True)
        for n, val in enumerate((mt + jnp.log(zt), ms + jnp.log(zs), dd / zt, tl)):
            m = jnp.where(lane == 4 * n + q, val, m)
        return m

    m = lax.fori_loop(0, 4, stats, jnp.zeros((Q, 128), f32))
    val = jnp.transpose(m)[:16]

    for axis, buf, at, number, rnd in (("gx", fx, 4 * g + x, 8, 4), ("y", fy, y, 4, 6), ("z", fz, z, 4, 7)):
        parts = spread(buf, axis, at, number, rnd, val)()

        def lse(lo):
            top = parts[0][lo : lo + 4]
            for p in parts[1:]:
                top = jnp.maximum(top, p[lo : lo + 4])
            es = [jnp.exp(p[lo : lo + 4] - top) for p in parts]
            tot = es[0]
            for e in es[1:]:
                tot = tot + e
            return top + jnp.log(tot), es, tot

        lse_t, es, tot = lse(0)
        lse_s, _, _ = lse(4)
        cross = es[0] * parts[0][8:12]
        tl = parts[0][12:16]
        for e, p in zip(es[1:], parts[1:]):
            cross = cross + e * p[8:12]
            tl = tl + p[12:16]
        val = jnp.concatenate([lse_t, lse_s, cross / tot, tl], axis=0)

    out[...] = val

    for k in range(3):
        tiny_copy((x + 1) % 4, k).wait_send()
        for c in colors:
            pay_copy(c, to(k), k).wait_send()
    for c in ends:
        c.wait_send()
    for c in colors:
        for n in range(3):
            first(c, n).wait_send()
        for n in range(4):
            second(c, n).wait_send()

    def drain(i, _):
        for c in colors:
            for n in range(4):
                third(c, n, i).wait_send()
                across(c, i, n).wait_send()
        return 0

    lax.fori_loop(0, 4, drain, 0)


def outputs(val_ref, counts, mask_time, out_kl, out_nll, out_loss):
    x = lax.axis_index("tok")
    lane256 = lax.broadcasted_iota(jnp.int32, (1, 256), 1)
    starts = []
    total = jnp.int32(0)
    for t in range(4):
        starts.append(total)
        total = total + counts[t]
    val = val_ref[...]
    lse_t, lse_s, cross, tl = (val[4 * n : 4 * n + 4] for n in range(4))
    kl = cross - lse_t + lse_s
    nll = lse_s - tl
    kl_total = jnp.sum(jnp.sum(kl, axis=1, keepdims=True), axis=0, keepdims=True)
    nll_total = jnp.sum(jnp.sum(nll, axis=1, keepdims=True), axis=0, keepdims=True)
    time = jnp.full((1, 1), mask_time[0], jnp.int32).astype(f32)
    masked = jnp.full((1, 1), total, jnp.int32).astype(f32)
    weight = 1000.0 / time
    out_loss[...] = jnp.concatenate([weight * nll_total / 8192.0, kl_total / masked], axis=1)

    cols = jnp.transpose(jnp.concatenate([kl, nll, jnp.zeros((120, 128), f32)], axis=0))
    start = jnp.int32(0)
    count = jnp.int32(0)
    for t in range(4):
        start = start + jnp.where(x == t, starts[t], 0)
        count = count + jnp.where(x == t, counts[t], 0)
    slot = lax.broadcasted_iota(jnp.int32, (Q, 256), 1)
    gap = lax.broadcasted_iota(jnp.int32, (Q, 256), 0) - slot
    for n, out in ((0, out_kl), (4, out_nll)):
        s = jnp.zeros((Q, 256), f32)
        for q in range(4):
            s = s + jnp.where(gap == start - q * Q, cols[:, n + q : n + q + 1], 0.0)
        s = jnp.sum(s, axis=0, keepdims=True)
        out[...] = jnp.where(lane256 < count, s, 0.0)


def shards(th, sh, tg, sg, wt, ws, targets, positions, counts, mask_time):
    vm = pl.BlockSpec(memory_space=pltpu.VMEM)
    sm = pl.BlockSpec(memory_space=pltpu.SMEM)
    anyspace = pl.BlockSpec(memory_space=pl.ANY)
    dma = pltpu.SemaphoreType.DMA
    val = pl.pallas_call(
        body,
        out_shape=jax.ShapeDtypeStruct((16, 128), f32),
        in_specs=[anyspace, anyspace, anyspace, vm, anyspace, anyspace, anyspace, anyspace, sm],
        out_specs=vm,
        scratch_shapes=[
            pltpu.VMEM((2048, 256), bf16),
            pltpu.VMEM((160, 2048), bf16),
            pltpu.VMEM((2, 128), bf16),
            pltpu.VMEM((64, 128), jnp.int32),
            pltpu.VMEM((8, 128), jnp.int32),
            pltpu.VMEM((ROWS, 2048), bf16),
            pltpu.VMEM((DT, NV), bf16),
            pltpu.VMEM((DS, NV), bf16),
            pltpu.VMEM((2, 4, 4, 4, XT, 128), bf16),
            pltpu.VMEM((2, 4, 4, 4, 128, 128), bf16),
            pltpu.VMEM((2, 4, 4, 4, XT, 128), bf16),
            pltpu.VMEM((ROWS, NV), f32),
            pltpu.VMEM((ROWS, NV), f32),
            pltpu.VMEM((4, Q, 1), f32),
            pltpu.VMEM((4, Q, 1), f32),
            pltpu.VMEM((4, Q, 1), f32),
            pltpu.VMEM((4, Q, 1), f32),
            pltpu.VMEM((4, 128, 128), bf16),
            pltpu.VMEM((4, 128, 128), bf16),
            pltpu.VMEM((4, 160, 128), bf16),
            pltpu.VMEM((4, 128, 128), bf16),
            pltpu.VMEM((4, 128, 128), bf16),
            pltpu.VMEM((4, 160, 128), bf16),
            pltpu.VMEM((8, 8, 128), f32),
            pltpu.VMEM((4, 8, 128), f32),
            pltpu.VMEM((4, 8, 128), f32),
            pltpu.VMEM((2, 8, 128), f32),
            pltpu.VMEM((4, 8, 128), f32),
            pltpu.VMEM((8, 16, 128), f32),
            pltpu.VMEM((4, 16, 128), f32),
            pltpu.VMEM((4, 16, 128), f32),
            dma((13,)),
            dma((3, 3)),
            dma((3, 3)),
            dma((9, 7)),
            dma((9, 7)),
            dma((3, N_ICI)),
            dma((3, N_ICI)),
            dma((3, N_SIB)),
            dma((3, N_SIB)),
        ],
        compiler_params=pltpu.CompilerParams(
            collective_id=0, has_side_effects=True, vmem_limit_bytes=58 * 1024 * 1024),
        name="elbo",
    )(
        th, sh.T, tg.reshape(2, 128), sg, wt, ws,
        targets.reshape(64, 128), positions.reshape(8, 128), counts,
    )
    kl, nll, loss = pl.pallas_call(
        outputs,
        out_shape=(
            jax.ShapeDtypeStruct((1, 256), f32),
            jax.ShapeDtypeStruct((1, 256), f32),
            jax.ShapeDtypeStruct((1, 2), f32),
        ),
        in_specs=[vm, sm, sm],
        out_specs=(vm, vm, vm),
        name="slots",
    )(val, counts, mask_time)
    return kl.reshape(256), nll.reshape(256), loss.reshape(2)


def solution(mesh):
    feats = ("group", "vocab")
    cols = ("group", "tok", "vocab")
    in_specs = (
        P("tok", feats), P("tok", feats), P(feats), P(feats),
        P(None, cols), P(None, cols), P(), P(), P(), P(),
    )
    out_specs = (P("tok"), P("tok"), P())
    return jax.shard_map(shards, mesh=mesh, in_specs=in_specs, out_specs=out_specs, check_vma=False)
```

time: 116 us -> 76 us (0.66)
  Pallas kernels: 106 us -> 74.5 us
  local copies, waits for them, and re-layouts: 8.28 us -> 0 us
    pallas_call x1 -> x2, Pallas kernels: 106 us -> 74.5 us  [the longest x1 72.8 us: shards(): pl.pallas_call(body, out_shape=jax.ShapeDtypeStruct((16, 128), f32), in_s...]
    unnamed x4 -> x0, local copies, waits for them, and re-layouts: 5.84 us -> none
    reshape x2 -> x0, local copies, waits for them, and re-layouts: 2.44 us -> none  [the longest x1 1.22 us: shards(): tg.reshape(1, 256)]
where the time goes in v2:
time: 76 us; the launch traced here: 75.8 us
  Pallas kernels  74.5 us (98%)
  between operations  1.29 us (2%)
    pallas_call x1, Pallas kernels, shards(): pl.pallas_call(body, out_shape=jax.ShapeDtypeStruct((16, 128), f32), in_s...  72.8 us
    pallas_call x1, Pallas kernels, shards(): pl.pallas_call(outputs, out_shape=(jax.ShapeDtypeStruct((1, 256), f32), j...  1.7 us

profile of v2, /device:TPU:0, one launch (start us, length us, event | category | flops | bytes accessed | tf_op | source)
XLA Modules:
  0.0 75.8 jit_solution(4484682629701393620)
XLA Ops:
  1.3 72.8 %elbo.1.val_ref = f32[16,128]{1,0:T(8,128)} custom-call(bf16[2048,256]{1,0:T(8,128)(2,1)} %th.1, bf16[160,2048]{1,0:T(8,128)(2,1)} %bitcast.7, bf16[2,128]{1,0:T(2,128)(2,1)} %bitcast.10, bf16[160]{0:T(256)(128)(2,1)} %sg.1, bf16[8192,768]{1,0:T(8,128)(2,1)} %wt_hbm.1, bf16[5120,768]{1,0:T(8,128)(2,1)} %ws_hbm.1, s32[64,128]{1,0:T(8,128)} %bitcast.8, ...), custom_call_target="tpu_custom_call" | custom-call | tf_op jit(solution)/shard_map/elbo/pallas_call | solution.py:544
  74.1 1.7 %slots.1 = (f32[1,256]{1,0:T(1,128)}, f32[1,256]{1,0:T(1,128)}, f32[1,2]{1,0:T(1,128)}) custom-call(f32[16,128]{1,0:T(8,128)} %elbo.1.val_ref, s32[4]{0:T(128)} %counts.3, s32[1]{0:T(128)S(6)} %copy.13.mask_time), custom_call_target="tpu_custom_call" | custom-call | tf_op jit(solution)/shard_map/slots/pallas_call | solution.py:598

commit v3 on v2

--- a/solution.py
+++ b/solution.py
@@ -32,7 +32,7 @@
     th, sh, tg_any, sg, wt_hbm, ws_hbm, targets_any, positions_any, counts,
     out,
     ht, hs, tg, targets, positions, hot, wt, ws, xa, xb, xc, acc_t, acc_s, tok_col, tgt_col,
-    sc_t, sc_s, pay_a, pay_b, pay_c, p1a, p1b, p1c, tx, tz, ty, tgp, txx, fx, fy, fz,
+    sc_t, sc_s, pay_a, pay_b, pay_c, p1a, p1b, p1c, tx, tz, ty, tgp, txx, fx, fy,
     load_sem, p1_s, p1_r, rnd_s, rnd_r, ici_s, ici_r, sib_s, sib_r,
 ):
     g = lax.axis_index("group")
@@ -49,8 +49,11 @@
             return {"vocab": ((y + k) % 4) * 4 + z}
         return {"vocab": y * 4 + (z + k) % 4}
 
+    def at_plane(k):
+        return {"vocab": ((y + k // 4) % 4) * 4 + (z + k % 4) % 4}
+
     barrier = pltpu.get_barrier_semaphore()
-    peers = [at_axis(a, k) for a in "xyz" for k in (1, 2, 3)] + [sib]
+    peers = [at_axis("x", k) for k in (1, 2, 3)] + [at_plane(k) for k in range(1, 16)] + [sib]
     peers += [{"group": 1 - g, "tok": (x + k) % 4} for k in (1, 2, 3)]
     for d in peers:
         pl.semaphore_signal(barrier, inc=1, device_id=d, device_id_type=MESH)
@@ -102,7 +105,7 @@
 
     def tiny_copy(q, k):
         return pltpu.make_async_remote_copy(
-            src_ref=tx.at[4 + q], dst_ref=tx.at[x], send_sem=rnd_s.at[0, k], recv_sem=rnd_r.at[0, k],
+            src_ref=tx.at[4 + q], dst_ref=tx.at[x], send_sem=rnd_s.at[0], recv_sem=rnd_r.at[k],
             device_id={"tok": q}, device_id_type=MESH)
 
     pays = ((pay_a, p1a), (pay_b, p1b), (pay_c, p1c))
@@ -110,7 +113,7 @@
     def pay_copy(c, q, k):
         src, dst = pays[c]
         return pltpu.make_async_remote_copy(
-            src_ref=src.at[q], dst_ref=dst.at[x], send_sem=p1_s.at[c, k], recv_sem=p1_r.at[c, k],
+            src_ref=src.at[q], dst_ref=dst.at[x], send_sem=p1_s.at[c], recv_sem=p1_r.at[c, k],
             device_id={"tok": q}, device_id_type=MESH)
 
     def to(k):
@@ -153,26 +156,26 @@
 
     ends = []
 
+    used = [3]
+
     def spread(buf, axis, at, number, rnd, value):
         buf[at] = value
-        if axis == "gx":
+        if axis == "g":
+            devs = [sib]
+        elif axis == "gx":
             devs = [sib] + [at_axis("x", k) for k in (1, 3, 2)]
             devs += [{"group": 1 - g, "tok": (x + k) % 4} for k in (1, 3, 2)]
-            cps = [pltpu.make_async_remote_copy(
-                src_ref=buf.at[at], dst_ref=buf.at[at], send_sem=rnd_s.at[rnd, n], recv_sem=rnd_r.at[rnd, n],
-                device_id=d, device_id_type=MESH) for n, d in enumerate(devs)]
-        elif axis == "g":
-            cps = [pltpu.make_async_remote_copy(
-                src_ref=buf.at[at], dst_ref=buf.at[at], send_sem=rnd_s.at[rnd, 0], recv_sem=rnd_r.at[rnd, 0],
-                device_id=sib, device_id_type=MESH)]
+        elif axis == "yz":
+            devs = [at_plane(k) for k in range(1, 16)]
         else:
-            cps = [pltpu.make_async_remote_copy(
-                src_ref=buf.at[at], dst_ref=buf.at[at], send_sem=rnd_s.at[rnd, k - 1],
-                recv_sem=rnd_r.at[rnd, k - 1], device_id=at_axis(axis, k), device_id_type=MESH)
-                for k in (1, 3, 2)]
+            devs = [at_axis(axis, k) for k in (1, 3, 2)]
+        cps = [pltpu.make_async_remote_copy(
+            src_ref=buf.at[at], dst_ref=buf.at[at], send_sem=rnd_s.at[rnd], recv_sem=rnd_r.at[used[0] + n],
+            device_id=d, device_id_type=MESH) for n, d in enumerate(devs)]
+        used[0] += len(devs)
         for c in cps:
             c.start()
-        ends.extend(cps)
+        ends.append((buf.at[0 : len(devs)], rnd_s.at[rnd]))
 
         def finish():
             for c in cps:
@@ -232,41 +235,41 @@
     def coords(c):
         return [here[a] for a in order[c]]
 
-    def ici(c, n, ref, axis, k):
+    def ici(c, stage, n, ref, axis, k):
         return pltpu.make_async_remote_copy(
-            src_ref=ref, dst_ref=ref, send_sem=ici_s.at[c, n], recv_sem=ici_r.at[c, n],
+            src_ref=ref, dst_ref=ref, send_sem=ici_s.at[c, stage], recv_sem=ici_r.at[c, n],
             device_id=at_axis(axis, k), device_id_type=MESH)
 
     def sibling(c, n, ref):
         return pltpu.make_async_remote_copy(
-            src_ref=ref, dst_ref=ref, send_sem=sib_s.at[c, n], recv_sem=sib_r.at[c, n],
+            src_ref=ref, dst_ref=ref, send_sem=sib_s.at[c], recv_sem=sib_r.at[c, n],
             device_id=sib, device_id_type=MESH)
 
     def first(c, n):
-        return ici(c, n, box(c, *coords(c)), order[c][0], (1, 3, 2)[n])
+        return ici(c, 0, n, box(c, *coords(c)), order[c][0], (1, 3, 2)[n])
 
     def second(c, n):
         a1, a2, a3 = coords(c)
         axis = order[c][1]
         if n == 0:
-            return ici(c, 4, box(c, everything, a2, a3), axis, 1)
+            return ici(c, 1, 4, box(c, everything, a2, a3), axis, 1)
         if n == 1:
-            return ici(c, 5, box(c, everything, a2, a3), axis, 3)
+            return ici(c, 1, 5, box(c, everything, a2, a3), axis, 3)
         if n == 2:
-            return ici(c, 6, box(c, pl.ds(0, 2), (a2 + 3) % 4, a3), axis, 1)
-        return ici(c, 7, box(c, pl.ds(2, 2), (a2 + 1) % 4, a3), axis, 3)
+            return ici(c, 1, 6, box(c, pl.ds(0, 2), (a2 + 3) % 4, a3), axis, 1)
+        return ici(c, 1, 7, box(c, pl.ds(2, 2), (a2 + 1) % 4, a3), axis, 3)
 
     def third(c, n, i):
         a1, a2, a3 = coords(c)
         axis = order[c][2]
         b2 = (a2 + off(i)) % 4
         if n == 0:
-            return ici(c, 8 + i, box(c, everything, b2, a3), axis, 1)
+            return ici(c, 2, 8 + i, box(c, everything, b2, a3), axis, 1)
         if n == 1:
-            return ici(c, 12 + i, box(c, everything, b2, a3), axis, 3)
+            return ici(c, 2, 12 + i, box(c, everything, b2, a3), axis, 3)
         if n == 2:
-            return ici(c, 16 + i, box(c, pl.ds(0, 2), b2, (a3 + 3) % 4), axis, 1)
-        return ici(c, 20 + i, box(c, pl.ds(2, 2), b2, (a3 + 1) % 4), axis, 3)
+            return ici(c, 2, 16 + i, box(c, pl.ds(0, 2), b2, (a3 + 3) % 4), axis, 1)
+        return ici(c, 2, 20 + i, box(c, pl.ds(2, 2), b2, (a3 + 1) % 4), axis, 3)
 
     def across(c, i, k):
         a1, a2, a3 = coords(c)
@@ -328,7 +331,7 @@
         third(c, 0, 3).start()
         third(c, 1, 3).start()
         across(c, 3, 0).start()
-    finish = spread(txx, "x", x, 4, 8, add_up(finish()))
+    finish = spread(txx, "x", x, 4, 4, add_up(finish()))
 
     def add(acc, xs, w, rows_of):
         xs = jnp.concatenate(xs, axis=1)
@@ -391,15 +394,15 @@
         @pl.when(i < 4)
         def _():
             for c in colors:
+                across(c, i, 0).wait_recv()
+            multiply(i, (0,))
+            for c in colors:
                 third(c, 0, i).wait_recv()
                 third(c, 2, i).start()
                 third(c, 1, i).wait_recv()
                 third(c, 3, i).start()
                 across(c, i, 3).start()
                 across(c, i, 1).start()
-            for c in colors:
-                across(c, i, 0).wait_recv()
-            multiply(i, (0,))
 
         @pl.when((i > 0) & (i < 4))
         def _():
@@ -455,7 +458,7 @@
     m = lax.fori_loop(0, 4, stats, jnp.zeros((Q, 128), f32))
     val = jnp.transpose(m)[:16]
 
-    for axis, buf, at, number, rnd in (("gx", fx, 4 * g + x, 8, 4), ("y", fy, y, 4, 6), ("z", fz, z, 4, 7)):
+    for axis, buf, at, number, rnd in (("gx", fx, 4 * g + x, 8, 5), ("yz", fy, v, 16, 6)):
         parts = spread(buf, axis, at, number, rnd, val)()
 
         def lse(lo):
@@ -479,26 +482,18 @@
 
     out[...] = val
 
-    for k in range(3):
-        tiny_copy((x + 1) % 4, k).wait_send()
-        for c in colors:
-            pay_copy(c, to(k), k).wait_send()
-    for c in ends:
-        c.wait_send()
-    for c in colors:
-        for n in range(3):
-            first(c, n).wait_send()
-        for n in range(4):
-            second(c, n).wait_send()
-
-    def drain(i, _):
-        for c in colors:
-            for n in range(4):
-                third(c, n, i).wait_send()
-                across(c, i, n).wait_send()
-        return 0
-
-    lax.fori_loop(0, 4, drain, 0)
+    def left(ref, sem):
+        pltpu.make_async_copy(ref, ref, sem).wait()
+
+    left(tx.at[0:3], rnd_s.at[0])
+    for ref, sem in ends:
+        left(ref, sem)
+    for c, ref in enumerate((xa, xb, xc)):
+        left(pays[c][0].at[0:3], p1_s.at[c])
+        left(ref.at[0, 0, 0, 0:3], ici_s.at[c, 0])
+        left(ref.at[0, 0, 0:3], ici_s.at[c, 1])
+        left(ref.at[0, 0:3], ici_s.at[c, 2])
+        left(ref.at[0], sib_s.at[c])
 
 
 def outputs(val_ref, counts, mask_time, out_kl, out_nll, out_loss):
@@ -576,16 +571,15 @@
             pltpu.VMEM((2, 8, 128), f32),
             pltpu.VMEM((4, 8, 128), f32),
             pltpu.VMEM((8, 16, 128), f32),
-            pltpu.VMEM((4, 16, 128), f32),
-            pltpu.VMEM((4, 16, 128), f32),
+            pltpu.VMEM((16, 16, 128), f32),
             dma((13,)),
+            dma((3,)),
             dma((3, 3)),
+            dma((7,)),
+            dma((35,)),
             dma((3, 3)),
-            dma((9, 7)),
-            dma((9, 7)),
             dma((3, N_ICI)),
-            dma((3, N_ICI)),
-            dma((3, N_SIB)),
+            dma((3,)),
             dma((3, N_SIB)),
         ],
         compiler_params=pltpu.CompilerParams(

time: 76 us -> 72.6 us (0.955)
  Pallas kernels: 74.5 us -> 71.1 us
    pallas_call x1, Pallas kernels: 72.8 us -> 69.4 us  [shards(): pl.pallas_call(body, out_shape=jax.ShapeDtypeStruct((16, 128), f32), in_s...]
where the time goes in v3:
time: 72.6 us; the launch traced here: 72.4 us
  Pallas kernels  71.1 us (98%)
  between operations  1.29 us (2%)
    pallas_call x1, Pallas kernels, shards(): pl.pallas_call(body, out_shape=jax.ShapeDtypeStruct((16, 128), f32), in_s...  69.4 us
    pallas_call x1, Pallas kernels, shards(): pl.pallas_call(outputs, out_shape=(jax.ShapeDtypeStruct((1, 256), f32), j...  1.7 us

profile of v3, /device:TPU:0, one launch (start us, length us, event | category | flops | bytes accessed | tf_op | source)
XLA Modules:
  0.0 72.4 jit_solution(12451135604905245855)
XLA Ops:
  1.3 69.4 %elbo.1.val_ref = f32[16,128]{1,0:T(8,128)} custom-call(bf16[2048,256]{1,0:T(8,128)(2,1)} %th.1, bf16[160,2048]{1,0:T(8,128)(2,1)} %bitcast.7, bf16[2,128]{1,0:T(2,128)(2,1)} %bitcast.10, bf16[160]{0:T(256)(128)(2,1)} %sg.1, bf16[8192,768]{1,0:T(8,128)(2,1)} %wt_hbm.1, bf16[5120,768]{1,0:T(8,128)(2,1)} %ws_hbm.1, s32[64,128]{1,0:T(8,128)} %bitcast.8, ...), custom_call_target="tpu_custom_call" | custom-call | tf_op jit(solution)/shard_map/elbo/pallas_call | solution.py:539
  70.7 1.7 %slots.1 = (f32[1,256]{1,0:T(1,128)}, f32[1,256]{1,0:T(1,128)}, f32[1,2]{1,0:T(1,128)}) custom-call(f32[16,128]{1,0:T(8,128)} %elbo.1.val_ref, s32[4]{0:T(128)} %counts.3, s32[1]{0:T(128)S(6)} %copy.13.mask_time), custom_call_target="tpu_custom_call" | custom-call | tf_op jit(solution)/shard_map/slots/pallas_call | solution.py:592

commit v4 on v3

--- a/solution.py
+++ b/solution.py
@@ -13,6 +13,7 @@
 bf16 = jnp.bfloat16
 
 ROWS = 512
+PLANE = (10, 6, 14, 9, 11, 2, 8, 5, 7, 13, 15, 1, 3, 4, 12)
 Q = 128
 DT = 8192
 DS = 5120
@@ -117,7 +118,7 @@
             device_id={"tok": q}, device_id_type=MESH)
 
     def to(k):
-        return (x + 1 + jnp.where(k == 1, 2, jnp.where(k == 2, 1, k))) % 4
+        return (x + (2, 1, 3)[k]) % 4
 
     def make_hot(q, _):
         tok = tok_col[q].astype(jnp.int32) - 2048 * x
@@ -163,12 +164,12 @@
         if axis == "g":
             devs = [sib]
         elif axis == "gx":
-            devs = [sib] + [at_axis("x", k) for k in (1, 3, 2)]
-            devs += [{"group": 1 - g, "tok": (x + k) % 4} for k in (1, 3, 2)]
+            devs = [{"group": 1 - g, "tok": (x + k) % 4} for k in (2, 1, 3)]
+            devs += [at_axis("x", k) for k in (2, 1, 3)] + [sib]
         elif axis == "yz":
-            devs = [at_plane(k) for k in range(1, 16)]
+            devs = [at_plane(k) for k in PLANE]
         else:
-            devs = [at_axis(axis, k) for k in (1, 3, 2)]
+            devs = [at_axis(axis, k) for k in (2, 1, 3)]
         cps = [pltpu.make_async_remote_copy(
             src_ref=buf.at[at], dst_ref=buf.at[at], send_sem=rnd_s.at[rnd], recv_sem=rnd_r.at[used[0] + n],
             device_id=d, device_id_type=MESH) for n, d in enumerate(devs)]
@@ -246,7 +247,7 @@
             device_id=sib, device_id_type=MESH)
 
     def first(c, n):
-        return ici(c, 0, n, box(c, *coords(c)), order[c][0], (1, 3, 2)[n])
+        return ici(c, 0, n, box(c, *coords(c)), order[c][0], (2, 1, 3)[n])
 
     def second(c, n):
         a1, a2, a3 = coords(c)
@@ -312,26 +313,28 @@
         third(c, 1, 0).start()
         across(c, 0, 0).start()
     finish = spread(ty, "y", y, 4, 2, add_up(finish()))
-    for c in colors:
-        second(c, 0).wait_recv()
-        second(c, 2).start()
-        second(c, 1).wait_recv()
-        second(c, 3).start()
-    for c in colors:
-        for i in (1, 2):
-            third(c, 0, i).start()
-            third(c, 1, i).start()
-            across(c, i, 0).start()
-    finish = spread(tgp, "g", g, 2, 3, add_up(finish()))
+    def near():
+        for c in colors:
+            second(c, 0).wait_recv()
+            second(c, 2).start()
+            second(c, 1).wait_recv()
+            second(c, 3).start()
+        for c in colors:
+            for i in (1, 2):
+                third(c, 0, i).start()
+                third(c, 1, i).start()
+                across(c, i, 0).start()
+
+    def far():
+        for c in colors:
+            second(c, 2).wait_recv()
+            second(c, 3).wait_recv()
+            third(c, 0, 3).start()
+            third(c, 1, 3).start()
+            across(c, 3, 0).start()
+
     for c in loads[2:]:
         c.wait()
-    for c in colors:
-        second(c, 2).wait_recv()
-        second(c, 3).wait_recv()
-        third(c, 0, 3).start()
-        third(c, 1, 3).start()
-        across(c, 3, 0).start()
-    finish = spread(txx, "x", x, 4, 4, add_up(finish()))
 
     def add(acc, xs, w, rows_of):
         xs = jnp.concatenate(xs, axis=1)
@@ -384,51 +387,63 @@
                 rows_of += [pl.ds(pl.multiple_of(chunk(*a) * 160 + 144, 16), 16) for a in at]
         add(acc_s.at[pl.ds(pl.multiple_of(x_i * Q, Q), Q)], xs, ws, rows_of)
 
-    def step(i, _):
-        def opposite(j):
-            for c in colors:
-                third(c, 2, j).wait_recv()
-                third(c, 3, j).wait_recv()
-                across(c, j, 2).start()
-
-        @pl.when(i < 4)
+    def step(e, _):
+        @pl.when(e < 4)
         def _():
             for c in colors:
-                across(c, i, 0).wait_recv()
-            multiply(i, (0,))
+                across(c, e, 0).wait_recv()
+            multiply(e, (0,))
+
+        @pl.when(e == 0)
+        def _():
+            near()
+
+        @pl.when((e > 0) & (e < 5))
+        def _():
+            i = e - 1
             for c in colors:
                 third(c, 0, i).wait_recv()
                 third(c, 2, i).start()
                 third(c, 1, i).wait_recv()
                 third(c, 3, i).start()
+            for c in colors:
                 across(c, i, 3).start()
                 across(c, i, 1).start()
 
-        @pl.when((i > 0) & (i < 4))
+        @pl.when(e == 1)
         def _():
-            opposite(i - 1)
-
-        @pl.when((i > 0) & (i < 5))
+            far()
+
+        @pl.when((e > 1) & (e < 6))
         def _():
+            i = e - 2
             for c in colors:
                 for k in (1, 3):
-                    across(c, i - 1, k).wait_recv()
-            multiply(i - 1, (1, 3))
-
-        @pl.when(i > 1)
+                    across(c, i, k).wait_recv()
+            multiply(i, (1, 3))
+
+        @pl.when((e > 2) & (e < 7))
         def _():
+            i = e - 3
             for c in colors:
-                across(c, i - 2, 2).wait_recv()
-            multiply(i - 2, (2,))
-            multiply_rest(i - 2)
-
-        @pl.when(i == 4)
+                third(c, 2, i).wait_recv()
+                third(c, 3, i).wait_recv()
+                across(c, i, 2).start()
+
+        @pl.when(e > 3)
         def _():
-            opposite(3)
+            i = e - 4
+            for c in colors:
+                across(c, i, 2).wait_recv()
+            multiply(i, (2,))
+            multiply_rest(i)
 
         return 0
 
-    lax.fori_loop(0, 6, step, 0)
+    lax.fori_loop(0, 2, step, 0)
+    finish = spread(tgp, "g", g, 2, 3, add_up(finish()))
+    finish = spread(txx, "x", x, 4, 4, add_up(finish()))
+    lax.fori_loop(2, 8, step, 0)
 
     parts = finish()
     width = jnp.where(lax.broadcasted_iota(jnp.int32, (8, 128), 0) % 2 == 0, float(DT), float(DS))

time: 72.6 us -> 66.6 us (0.917)
  Pallas kernels: 71.1 us -> 65.1 us
    pallas_call x1, Pallas kernels: 69.4 us -> 63.4 us  [shards(): pl.pallas_call(body, out_shape=jax.ShapeDtypeStruct((16, 128), f32), in_s...]
where the time goes in v4:
time: 66.6 us; the launch traced here: 66.4 us
  Pallas kernels  65.1 us (98%)
  between operations  1.29 us (2%)
    pallas_call x1, Pallas kernels, shards(): pl.pallas_call(body, out_shape=jax.ShapeDtypeStruct((16, 128), f32), in_s...  63.4 us
    pallas_call x1, Pallas kernels, shards(): pl.pallas_call(outputs, out_shape=(jax.ShapeDtypeStruct((1, 256), f32), j...  1.7 us

profile of v4, /device:TPU:0, one launch (start us, length us, event | category | flops | bytes accessed | tf_op | source)
XLA Modules:
  0.0 66.4 jit_solution(14972838906582154712)
XLA Ops:
  1.3 63.4 %elbo.1.val_ref = f32[16,128]{1,0:T(8,128)} custom-call(bf16[2048,256]{1,0:T(8,128)(2,1)} %th.1, bf16[160,2048]{1,0:T(8,128)(2,1)} %bitcast.7, bf16[2,128]{1,0:T(2,128)(2,1)} %bitcast.10, bf16[160]{0:T(256)(128)(2,1)} %sg.1, bf16[8192,768]{1,0:T(8,128)(2,1)} %wt_hbm.1, bf16[5120,768]{1,0:T(8,128)(2,1)} %ws_hbm.1, s32[64,128]{1,0:T(8,128)} %bitcast.8, ...), custom_call_target="tpu_custom_call" | custom-call | tf_op jit(solution)/shard_map/elbo/pallas_call | solution.py:554
  64.7 1.7 %slots.1 = (f32[1,256]{1,0:T(1,128)}, f32[1,256]{1,0:T(1,128)}, f32[1,2]{1,0:T(1,128)}) custom-call(f32[16,128]{1,0:T(8,128)} %elbo.1.val_ref, s32[4]{0:T(128)} %counts.3, s32[1]{0:T(128)S(6)} %copy.13.mask_time), custom_call_target="tpu_custom_call" | custom-call | tf_op jit(solution)/shard_map/slots/pallas_call | solution.py:607

commit v5 on v4

--- a/solution.py
+++ b/solution.py
@@ -56,9 +56,6 @@
     barrier = pltpu.get_barrier_semaphore()
     peers = [at_axis("x", k) for k in (1, 2, 3)] + [at_plane(k) for k in range(1, 16)] + [sib]
     peers += [{"group": 1 - g, "tok": (x + k) % 4} for k in (1, 2, 3)]
-    for d in peers:
-        pl.semaphore_signal(barrier, inc=1, device_id=d, device_id_type=MESH)
-
     small = [
         pltpu.make_async_copy(positions_any, positions, load_sem.at[10]),
         pltpu.make_async_copy(tg_any, tg, load_sem.at[11]),
@@ -73,8 +70,10 @@
         loads.append(pltpu.make_async_copy(wt_hbm.at[r], wt.at[r], load_sem.at[2 + i]))
         r = pl.ds(i * (DS // 4), DS // 4)
         loads.append(pltpu.make_async_copy(ws_hbm.at[r], ws.at[r], load_sem.at[6 + i]))
-    for c in small + loads:
+    for c in small[:1] + loads[:2] + small[1:] + loads[2:]:
         c.start()
+    for d in peers:
+        pl.semaphore_signal(barrier, inc=1, device_id=d, device_id_type=MESH)
 
     starts = []
     total = jnp.int32(0)
@@ -135,8 +134,9 @@
         pay_a[q] = cq[:, :128].astype(bf16)
         pay_b[q] = cq[:, 128:].astype(bf16)
     pl.semaphore_wait(barrier, len(peers))
-    for k in range(3):
-        pay_copy(1, to(k), k).start()
+    for c in (1, 0):
+        for k in range(3):
+            pay_copy(c, to(k), k).start()
     loads[1].wait()
     cs = lax.dot_general(hot[...], hs[...], (((1,), (1,)), ((), ())), preferred_element_type=f32)
     for q in range(4):
@@ -152,9 +152,6 @@
         pay_copy(2, to(k), k).start()
     for k in range(3):
         tiny_copy(to(k), k).start()
-    for k in range(3):
-        pay_copy(0, to(k), k).start()
-
     ends = []
 
     used = [3]
@@ -299,7 +296,6 @@
         tgt_col[q] = ids
         return 0
 
-    lax.fori_loop(0, 4, find_targets, 0)
     acc_t[...] = jnp.zeros_like(acc_t)
     acc_s[...] = jnp.zeros_like(acc_s)
 
@@ -320,9 +316,10 @@
             second(c, 1).wait_recv()
             second(c, 3).start()
         for c in colors:
+            third(c, 0, 1).start()
+            third(c, 1, 1).start()
+        for c in colors:
             for i in (1, 2):
-                third(c, 0, i).start()
-                third(c, 1, i).start()
                 across(c, i, 0).start()
 
     def far():
@@ -396,6 +393,7 @@
 
         @pl.when(e == 0)
         def _():
+            lax.fori_loop(0, 4, find_targets, 0)
             near()
 
         @pl.when((e > 0) & (e < 5))
@@ -409,6 +407,12 @@
             for c in colors:
                 across(c, i, 3).start()
                 across(c, i, 1).start()
+
+        @pl.when(e == 1)
+        def _():
+            for c in colors:
+                third(c, 0, 2).start()
+                third(c, 1, 2).start()
 
         @pl.when(e == 1)
         def _():

time: 66.6 us -> 64.8 us (0.973)
  Pallas kernels: 65.1 us -> 63.3 us
    pallas_call x1, Pallas kernels: 63.4 us -> 61.6 us  [shards(): pl.pallas_call(body, out_shape=jax.ShapeDtypeStruct((16, 128), f32), in_s...]
where the time goes in v5:
time: 64.8 us; the launch traced here: 64.6 us
  Pallas kernels  63.3 us (98%)
  between operations  1.29 us (2%)
    pallas_call x1, Pallas kernels, shards(): pl.pallas_call(body, out_shape=jax.ShapeDtypeStruct((16, 128), f32), in_s...  61.6 us
    pallas_call x1, Pallas kernels, shards(): pl.pallas_call(outputs, out_shape=(jax.ShapeDtypeStruct((1, 256), f32), j...  1.7 us

profile of v5, /device:TPU:0, one launch (start us, length us, event | category | flops | bytes accessed | tf_op | source)
XLA Modules:
  0.0 64.6 jit_solution(9363841307577066400)
XLA Ops:
  1.3 61.6 %elbo.1.val_ref = f32[16,128]{1,0:T(8,128)} custom-call(bf16[2048,256]{1,0:T(8,128)(2,1)} %th.1, bf16[160,2048]{1,0:T(8,128)(2,1)} %bitcast.7, bf16[2,128]{1,0:T(2,128)(2,1)} %bitcast.10, bf16[160]{0:T(256)(128)(2,1)} %sg.1, bf16[8192,768]{1,0:T(8,128)(2,1)} %wt_hbm.1, bf16[5120,768]{1,0:T(8,128)(2,1)} %ws_hbm.1, s32[64,128]{1,0:T(8,128)} %bitcast.8, ...), custom_call_target="tpu_custom_call" | custom-call | tf_op jit(solution)/shard_map/elbo/pallas_call | solution.py:558
  62.9 1.7 %slots.1 = (f32[1,256]{1,0:T(1,128)}, f32[1,256]{1,0:T(1,128)}, f32[1,2]{1,0:T(1,128)}) custom-call(f32[16,128]{1,0:T(8,128)} %elbo.1.val_ref, s32[4]{0:T(128)} %counts.3, s32[1]{0:T(128)S(6)} %copy.13.mask_time), custom_call_target="tpu_custom_call" | custom-call | tf_op jit(solution)/shard_map/slots/pallas_call | solution.py:611

commit v6 on v5

--- a/solution.py
+++ b/solution.py
@@ -33,7 +33,7 @@
     th, sh, tg_any, sg, wt_hbm, ws_hbm, targets_any, positions_any, counts,
     out,
     ht, hs, tg, targets, positions, hot, wt, ws, xa, xb, xc, acc_t, acc_s, tok_col, tgt_col,
-    sc_t, sc_s, pay_a, pay_b, pay_c, p1a, p1b, p1c, tx, tz, ty, tgp, txx, fx, fy,
+    sc_t, sc_s, pay_a, pay_b, pay_c, p1a, p1b, p1c, tx, tz, ty, txx, fx, fy,
     load_sem, p1_s, p1_r, rnd_s, rnd_r, ici_s, ici_r, sib_s, sib_r,
 ):
     g = lax.axis_index("group")
@@ -130,13 +130,15 @@
     ct = jnp.dot(hot[...], ht[...], preferred_element_type=f32)
     for q in range(4):
         cq = ct[q * Q : (q + 1) * Q]
-        sc_t[q] = jnp.sum(cq * cq, axis=1, keepdims=True)
         pay_a[q] = cq[:, :128].astype(bf16)
         pay_b[q] = cq[:, 128:].astype(bf16)
     pl.semaphore_wait(barrier, len(peers))
     for c in (1, 0):
         for k in range(3):
             pay_copy(c, to(k), k).start()
+    for q in range(4):
+        ca, cb = pay_a[q].astype(f32), pay_b[q].astype(f32)
+        sc_t[q] = jnp.sum(ca * ca + cb * cb, axis=1, keepdims=True)
     loads[1].wait()
     cs = lax.dot_general(hot[...], hs[...], (((1,), (1,)), ((), ())), preferred_element_type=f32)
     for q in range(4):
@@ -158,9 +160,7 @@
 
     def spread(buf, axis, at, number, rnd, value):
         buf[at] = value
-        if axis == "g":
-            devs = [sib]
-        elif axis == "gx":
+        if axis == "gx":
             devs = [{"group": 1 - g, "tok": (x + k) % 4} for k in (2, 1, 3)]
             devs += [at_axis("x", k) for k in (2, 1, 3)] + [sib]
         elif axis == "yz":
@@ -445,11 +445,11 @@
         return 0
 
     lax.fori_loop(0, 2, step, 0)
-    finish = spread(tgp, "g", g, 2, 3, add_up(finish()))
-    finish = spread(txx, "x", x, 4, 4, add_up(finish()))
+    finish = spread(txx, "gx", 4 * g + x, 8, 3, add_up(finish()))
     lax.fori_loop(2, 8, step, 0)
 
     parts = finish()
+    parts = [parts[i] + parts[4 + i] for i in range(4)]
     width = jnp.where(lax.broadcasted_iota(jnp.int32, (8, 128), 0) % 2 == 0, float(DT), float(DS))
     scale = lax.rsqrt(jnp.concatenate([p[0:2] for p in parts], axis=0) / width + EPS)
     scale = jnp.transpose(jnp.concatenate([scale, jnp.zeros((120, 128), f32)], axis=0))
@@ -587,15 +587,14 @@
             pltpu.VMEM((8, 8, 128), f32),
             pltpu.VMEM((4, 8, 128), f32),
             pltpu.VMEM((4, 8, 128), f32),
-            pltpu.VMEM((2, 8, 128), f32),
-            pltpu.VMEM((4, 8, 128), f32),
+            pltpu.VMEM((8, 8, 128), f32),
             pltpu.VMEM((8, 16, 128), f32),
             pltpu.VMEM((16, 16, 128), f32),
             dma((13,)),
             dma((3,)),
             dma((3, 3)),
             dma((7,)),
-            dma((35,)),
+            dma((38,)),
             dma((3, 3)),
             dma((3, N_ICI)),
             dma((3,)),

time: 64.8 us -> 64.8 us (level)
  no operation moved by 1% of the time
where the time goes in v6:
time: 64.8 us; the launch traced here: 64.6 us
  Pallas kernels  63.3 us (98%)
  between operations  1.29 us (2%)
    pallas_call x1, Pallas kernels, shards(): pl.pallas_call(body, out_shape=jax.ShapeDtypeStruct((16, 128), f32), in_s...  61.6 us
    pallas_call x1, Pallas kernels, shards(): pl.pallas_call(outputs, out_shape=(jax.ShapeDtypeStruct((1, 256), f32), j...  1.7 us

profile of v6, /device:TPU:0, one launch (start us, length us, event | category | flops | bytes accessed | tf_op | source)
XLA Modules:
  0.0 64.6 jit_solution(4955781741508359634)
XLA Ops:
  1.3 61.6 %elbo.1.val_ref = f32[16,128]{1,0:T(8,128)} custom-call(bf16[2048,256]{1,0:T(8,128)(2,1)} %th.1, bf16[160,2048]{1,0:T(8,128)(2,1)} %bitcast.7, bf16[2,128]{1,0:T(2,128)(2,1)} %bitcast.10, bf16[160]{0:T(256)(128)(2,1)} %sg.1, bf16[8192,768]{1,0:T(8,128)(2,1)} %wt_hbm.1, bf16[5120,768]{1,0:T(8,128)(2,1)} %ws_hbm.1, s32[64,128]{1,0:T(8,128)} %bitcast.8, ...), custom_call_target="tpu_custom_call" | custom-call | tf_op jit(solution)/shard_map/elbo/pallas_call | solution.py:558
  62.9 1.7 %slots.1 = (f32[1,256]{1,0:T(1,128)}, f32[1,256]{1,0:T(1,128)}, f32[1,2]{1,0:T(1,128)}) custom-call(f32[16,128]{1,0:T(8,128)} %elbo.1.val_ref, s32[4]{0:T(128)} %counts.3, s32[1]{0:T(128)S(6)} %copy.13.mask_time), custom_call_target="tpu_custom_call" | custom-call | tf_op jit(solution)/shard_map/slots/pallas_call | solution.py:610
